TPU v7x, 32 devices: a whole 2x2x4 slice. The times are simulated.
32 devices in a mesh: groups: 2 (over x), walk: 16 (over z, y, core).
Axes of the slice: x: 2, y: 2, z: 4, core: 2. Of those that a mesh axis runs over, the one named last changes fastest.
Arguments:
- walkers: bfloat16 [32, 768, 1536], P(('groups', 'walk')), parts along dimension 0, may hold values from -6 to 6
- theta: bfloat16 [32, 768, 1536], P(('groups', 'walk')), parts along dimension 0, may hold values from -0.21875 to 0.21875
- cholesky: float32 [32, 16, 4, 4096], P(('groups', 'walk')), parts along dimension 0, may hold values from -0.875 to 0.875
- tiles: int32 [32, 4], P('groups'), parts along dimension 0, may hold values from 0 to 575, as said below
- fields: float32 [2, 32, 256], P(None, ('groups', 'walk')), parts along dimension 1, may hold values from -5 to 5
- source: int32 [32], P('groups'), parts along dimension 0, may hold values from 0 to 15
Outputs:
- walkers_out: bfloat16 [32, 768, 1536], P(('groups', 'walk')), parts along dimension 0
- force_bias: float32 [2, 32, 256], P(None, ('groups', 'walk')), parts along dimension 1
There are 2 independent parts, one for each index of `groups`. A program takes and returns all parts, laid end to end along the dimension named above; each array names one. Nothing has to cross between parts.
Inputs may be any that keep to these rules, and one draw needn't show every extreme that they name: `tiles`: the 4 tile ids of one block are distinct.
All inputs are finite; a program needn't handle non-finite values.
Results may differ from a plain program's by a relative error of at most 0.0065.
Values may be sent and summed in bfloat16 or wider, within the bound.
A program may use at most 128 MiB of HBM per device.

v0:
```python
import jax
import jax.numpy as jnp
from jax import lax
from jax.sharding import PartitionSpec as P

TILE = 64


def local(walkers, theta, cholesky, tiles, fields, source):
    own_walkers, occupied, orbital_count = walkers.shape
    tile_rows = orbital_count // TILE
    block_count, tile_slots = tiles.shape
    vectors = cholesky.shape[1]
    flat_ids = tiles.reshape(-1)
    row_block = flat_ids // tile_rows
    col_block = flat_ids % tile_rows
    picks = block_count * tile_slots
    chol_flat = cholesky.reshape(vectors, tile_slots * TILE * TILE)
    local_fields = lax.all_to_all(fields, "walk", split_axis=2, concat_axis=1, tiled=True)
    orbitals = walkers
    collected = []
    for sweep in range(2):
        green = jnp.einsum(
            "wik,wil->wkl", theta, orbitals, preferred_element_type=jnp.float32
        ).astype(jnp.bfloat16)
        green = green.reshape(own_walkers, tile_rows, TILE, tile_rows, TILE)
        picked = green[:, row_block, :, col_block, :]
        picked = jnp.moveaxis(picked, 0, 1).reshape(
            own_walkers, block_count, tile_slots * TILE * TILE
        )
        arrived = lax.all_to_all(picked, "walk", split_axis=1, concat_axis=0, tiled=True)
        arrived = arrived.reshape(-1, tile_slots * TILE * TILE).astype(jnp.float32)
        bias_local = jnp.dot(arrived, chol_flat.T, precision=lax.Precision.HIGHEST)
        collected.append(bias_local)
        shift_local = local_fields[sweep] - jnp.clip(0.5 * bias_local, -1.0, 1.0)
        partial_value = (
            0.1 * jnp.dot(shift_local, chol_flat, precision=lax.Precision.HIGHEST)
        ).astype(jnp.bfloat16)
        partial_value = partial_value.reshape(-1, 1, tile_slots * TILE * TILE)
        returned = lax.all_to_all(partial_value, "walk", split_axis=0, concat_axis=1, tiled=True)
        returned = returned.reshape(own_walkers, picks, TILE, TILE).astype(jnp.float32)
        values = jnp.transpose(returned, (1, 0, 2, 3))
        dense = jnp.zeros((own_walkers, tile_rows, TILE, tile_rows, TILE), jnp.float32)
        dense = dense.at[:, row_block, :, col_block, :].add(values)
        potential = dense.astype(jnp.bfloat16).reshape(own_walkers, orbital_count, orbital_count)
        moved = jnp.einsum("wik,wkl->wil", orbitals, potential, preferred_element_type=jnp.float32)
        orbitals = (orbitals.astype(jnp.float32) + moved).astype(jnp.bfloat16)
    biases = lax.all_to_all(jnp.stack(collected), "walk", split_axis=1, concat_axis=2, tiled=True)
    row_shares = lax.all_to_all(orbitals, "walk", split_axis=1, concat_axis=0, tiled=True)
    chosen = jnp.take(row_shares, source, axis=0)
    walkers_out = lax.all_to_all(chosen, "walk", split_axis=0, concat_axis=1, tiled=True)
    return (walkers_out, biases)


def solution(mesh):
    in_specs = (
        P(("groups", "walk"), None, None),
        P(("groups", "walk"), None, None),
        P(("groups", "walk"), None, None, None),
        P("groups", None),
        P(None, ("groups", "walk"), None),
        P("groups"),
    )
    out_specs = (P(("groups", "walk"), None, None), P(None, ("groups", "walk"), None))
    return jax.shard_map(local, mesh=mesh, in_specs=in_specs, out_specs=out_specs, check_vma=False)
```

profile of v0, /device:TPU:13, one launch (start us, length us, event | category | flops | bytes accessed | tf_op | source)
XLA Modules:
  0.0 510.4 jit_solution(16699166196683472177)
XLA Ops:
  18.5 12.6 %reshape.225 = bf16[24,64,24,64]{3,2,1,0:T(8,128)(2,1)} reshape(bf16[1536,1536]{1,0:T(8,128)(2,1)} %convolution_convert_fusion.1) | data formatting | bytes 9437184 | tf_op jit(solution)/shard_map/reshape | solution.py:26
  31.2 10.0 %copy.65 = bf16[24,64,24,64]{3,1,2,0:T(8,128)(2,1)} copy(bf16[24,64,24,64]{3,2,1,0:T(8,128)(2,1)} %reshape.225) | data formatting | bytes 9437184 | tf_op jit(solution)/shard_map/reshape | solution.py:26
  68.7 8.0 %all-to-all-done.1 = bf16[16,2,8192]{2,1,0:T(2,128)(2,1)} async-done(((bf16[16,2,8192]{2,1,0:T(2,128)(2,1)}), bf16[16,2,8192]{2,1,0:T(2,128)(2,1)}, u32[]{:S(2)}, u32[]{:S(2)}) %all-to-all-start.1) | async-done | bytes 524320 | tf_op jit(solution)/shard_map/all_to_all | solution.py:31
  99.1 9.2 %all-to-all-done.2 = bf16[16,2,8192]{2,1,0:T(2,128)(2,1)} async-done(((bf16[16,2,8192]{2,1,0:T(2,128)(2,1)}), bf16[16,2,8192]{2,1,0:T(2,128)(2,1)}, u32[]{:S(2)}, u32[]{:S(2)}) %all-to-all-start.2) | async-done | bytes 524320 | tf_op jit(solution)/shard_map/all_to_all | solution.py:40
  120.4 8.9 %broadcast.176.clone = f32[24,64,24,64]{3,1,2,0:T(8,128)} broadcast(f32[]{:T(128)} %constant.38.clone.1), dimensions={} | broadcast | bytes 9437188 | tf_op jit(solution)/shard_map/broadcast.15
  129.3 10.9 %scatter_fusion = f32[24,64,24,64]{3,1,2,0:T(8,128)} fusion(f32[24,64,24,64]{3,1,2,0:T(8,128)} %broadcast.176.clone, s32[64]{0:T(128)S(1)} %fusion.32, f32[64,64,64]{2,1,0:T(8,128)} %reshape.255), kind=kCustom, calls=%fused_computation.3 | custom fusion | flops 262144 | bytes 3146240 | tf_op jit(solution)/shard_map/scatter-add | solution.py:44
  140.2 10.5 %convert_element_type.84 = bf16[24,64,24,64]{3,1,2,0:T(8,128)(2,1)} convert(f32[24,64,24,64]{3,1,2,0:T(8,128)} %scatter_fusion) | non-fusion elementwise | flops 2359296 | bytes 14155776 | tf_op jit(solution)/shard_map/convert_element_type | solution.py:45
  150.8 15.9 %copy.68 = bf16[24,64,24,64]{3,2,1,0:T(8,128)(2,1)} copy(bf16[24,64,24,64]{3,1,2,0:T(8,128)(2,1)} %convert_element_type.84) | data formatting | bytes 9437184 | tf_op jit(solution)/shard_map/convert_element_type | solution.py:45
  166.6 13.4 %reshape.217 = bf16[1536,1536]{1,0:T(8,128)(2,1)} reshape(bf16[24,64,24,64]{3,2,1,0:T(8,128)(2,1)} %copy.68) | data formatting | bytes 9437184 | tf_op jit(solution)/shard_map/reshape.29
  180.1 7.6 %fusion.5 = bf16[1,768,1536]{1,2,0:T(8,128)(2,1)S(1)} fusion(bf16[1,768,1536]{1,2,0:T(8,128)(2,1)} %copy.60, bf16[1536,1536]{1,0:T(8,128)(2,1)} %reshape.217, bf16[1,768,1536]{2,1,0:T(8,128)(2,1)} %param.6), kind=kOutput, calls=%fused_computation.15 | convolution fusion | flops 3627417600 | bytes 11796480 | tf_op jit(solution)/shard_map/wik,wkl->wil/dot_general | solution.py:46
  194.7 12.6 %reshape.233 = bf16[24,64,24,64]{1,0,3,2:T(8,128)(2,1)} reshape(bf16[1536,1536]{0,1:T(8,128)(2,1)} %fusion.4) | data formatting | bytes 9437184 | tf_op jit(solution)/shard_map/reshape | solution.py:26
  207.3 12.8 %copy.69 = bf16[24,64,24,64]{3,1,2,0:T(8,128)(2,1)} copy(bf16[24,64,24,64]{1,0,3,2:T(8,128)(2,1)} %reshape.233) | data formatting | bytes 9437184 | tf_op jit(solution)/shard_map/reshape | solution.py:26
  235.6 13.4 %all-to-all-done.3 = bf16[16,2,8192]{2,1,0:T(2,128)(2,1)S(1)} async-done(((bf16[16,2,8192]{2,1,0:T(2,128)(2,1)}), bf16[16,2,8192]{2,1,0:T(2,128)(2,1)S(1)}, u32[]{:S(2)}, u32[]{:S(2)}) %all-to-all-start.3) | async-done | bytes 524320 | tf_op jit(solution)/shard_map/all_to_all | solution.py:31
  253.3 18.4 %all_to_all.82 = bf16[16,2,8192]{2,1,0:T(2,128)(2,1)S(1)} all-to-all(bf16[16,2,8192]{2,1,0:T(2,128)(2,1)S(1)} %reshape.290), channel_id=1, replica_groups=mesh['groups'=2,'walk'=16] {'walk'}, dimensions={0} | all-to-all | bytes 1048576 | tf_op jit(solution)/shard_map/all_to_all | solution.py:40
  275.9 8.9 %broadcast.176 = f32[24,64,24,64]{3,1,2,0:T(8,128)} broadcast(f32[]{:T(128)} %constant.38.clone.1), dimensions={} | broadcast | bytes 9437188 | tf_op jit(solution)/shard_map/broadcast.15
  284.8 9.6 %scatter_fusion.1 = f32[24,64,24,64]{3,1,2,0:T(8,128)} fusion(f32[24,64,24,64]{3,1,2,0:T(8,128)} %broadcast.176, s32[64]{0:T(128)S(1)} %fusion.32, f32[64,64,64]{2,1,0:T(8,128)S(1)} %reshape.265), kind=kCustom, calls=%fused_computation.4 | custom fusion | flops 262144 | bytes 3146240 | tf_op jit(solution)/shard_map/scatter-add | solution.py:44
  294.4 10.5 %convert_element_type.85 = bf16[24,64,24,64]{3,1,2,0:T(8,128)(2,1)} convert(f32[24,64,24,64]{3,1,2,0:T(8,128)} %scatter_fusion.1) | non-fusion elementwise | flops 2359296 | bytes 14155776 | tf_op jit(solution)/shard_map/convert_element_type | solution.py:45
  305.0 15.9 %copy.72 = bf16[24,64,24,64]{3,2,1,0:T(8,128)(2,1)} copy(bf16[24,64,24,64]{3,1,2,0:T(8,128)(2,1)} %convert_element_type.85) | data formatting | bytes 9437184 | tf_op jit(solution)/shard_map/convert_element_type | solution.py:45
  320.9 13.3 %reshape.222 = bf16[1536,1536]{1,0:T(8,128)(2,1)} reshape(bf16[24,64,24,64]{3,2,1,0:T(8,128)(2,1)} %copy.72) | data formatting | bytes 9437184 | tf_op jit(solution)/shard_map/reshape.44
  334.1 7.7 %fusion.6 = bf16[1,768,1536]{1,2,0:T(8,128)(2,1)S(1)} fusion(bf16[1,768,1536]{1,2,0:T(8,128)(2,1)} %copy-done.4, bf16[1536,1536]{1,0:T(8,128)(2,1)} %reshape.222), kind=kOutput, calls=%fused_computation.17 | convolution fusion | flops 3627417600 | bytes 9437184 | tf_op jit(solution)/shard_map/wik,wkl->wil/dot_general | solution.py:46
  341.8 8.6 %copy.74 = bf16[1,768,1536]{2,0,1:T(2,128)(2,1)} copy(bf16[1,768,1536]{1,2,0:T(8,128)(2,1)S(1)} %fusion.6) | data formatting | bytes 4718592 | tf_op jit(solution)/shard_map/convert_element_type | solution.py:47
  350.4 15.7 %reduce.12 = bf16[768,1536]{1,0:T(8,128)(2,1)S(1)} reduce(bf16[768,1,1536]{2,1,0:T(2,128)(2,1)} %bitcast.70, bf16[]{:T(256)} %broadcast.209), dimensions={1}, to_apply=%bitcast.58.reduce_sub_computation | reduce | bytes 4718594
  374.8 52.4 %all-to-all-done.5 = bf16[16,2,36864]{2,1,0:T(2,128)(2,1)S(1)} async-done(((bf16[16,2,36864]{2,1,0:T(2,128)(2,1)}), bf16[16,2,36864]{2,1,0:T(2,128)(2,1)S(1)}, u32[]{:S(2)}, u32[]{:S(2)}) %all-to-all-start.5) | async-done | bytes 2359328 | tf_op jit(solution)/shard_map/all_to_all | solution.py:49
  454.1 52.5 %all-to-all-done.6 = bf16[16,48,1536]{2,1,0:T(8,128)(2,1)} async-done(((bf16[16,48,1536]{2,1,0:T(8,128)(2,1)}), bf16[16,48,1536]{2,1,0:T(8,128)(2,1)}, u32[]{:S(2)}, u32[]{:S(2)}) %all-to-all-start.6) | async-done | bytes 2359328 | tf_op jit(solution)/shard_map/all_to_all | solution.py:51
  (75 shorter events, 149.7 us)
Async XLA Ops:
  0.6 10.1 %copy-start = (bf16[1,768,1536]{2,1,0:T(8,128)(2,1)S(1)}, bf16[1,768,1536]{2,1,0:T(8,128)(2,1)}, u32[]{:S(2)}) copy-start(bf16[1,768,1536]{2,1,0:T(8,128)(2,1)} %param.7) | copy-start | bytes 7077892
  2.3 54.2 %all-to-all-start = ((f32[2,1,256]{0,1,2:T(1,128)}), f32[2,1,256]{0,1,2:T(1,128)S(1)}, u32[]{:S(2)}, u32[]{:S(2)}) async-start(f32[2,1,256]{0,1,2:T(1,128)} %copy.64), calls=%async_computation | async-start | bytes 262144 | tf_op jit(solution)/shard_map/all_to_all | solution.py:19
  56.5 20.2 %all-to-all-start.1 = ((bf16[16,2,8192]{2,1,0:T(2,128)(2,1)}), bf16[16,2,8192]{2,1,0:T(2,128)(2,1)}, u32[]{:S(2)}, u32[]{:S(2)}) async-start(bf16[16,2,8192]{2,1,0:T(2,128)(2,1)} %reshape.284), calls=%async_computation.1 | async-start | bytes 1048576 | tf_op jit(solution)/shard_map/all_to_all | solution.py:31
  89.5 18.8 %all-to-all-start.2 = ((bf16[16,2,8192]{2,1,0:T(2,128)(2,1)}), bf16[16,2,8192]{2,1,0:T(2,128)(2,1)}, u32[]{:S(2)}, u32[]{:S(2)}) async-start(bf16[16,2,8192]{2,1,0:T(2,128)(2,1)} %reshape.286), calls=%async_computation.2 | async-start | bytes 1048576 | tf_op jit(solution)/shard_map/all_to_all | solution.py:40
  94.8 4.3 copy-start.2
  187.7 1.4 copy-start.4
  230.3 18.7 %all-to-all-start.3 = ((bf16[16,2,8192]{2,1,0:T(2,128)(2,1)}), bf16[16,2,8192]{2,1,0:T(2,128)(2,1)S(1)}, u32[]{:S(2)}, u32[]{:S(2)}) async-start(bf16[16,2,8192]{2,1,0:T(2,128)(2,1)} %reshape.288), calls=%async_computation.3 | async-start | bytes 1048576 | tf_op jit(solution)/shard_map/all_to_all | solution.py:31
  369.0 5.1 %copy-start.3 = (s32[16]{0:T(128)S(1)}, s32[16]{0:T(128)}, u32[]{:S(2)}) copy-start(s32[16]{0:T(128)} %param.11) | copy-start | bytes 196
  369.0 58.1 %all-to-all-start.5 = ((bf16[16,2,36864]{2,1,0:T(2,128)(2,1)}), bf16[16,2,36864]{2,1,0:T(2,128)(2,1)S(1)}, u32[]{:S(2)}, u32[]{:S(2)}) async-start(bf16[16,2,36864]{2,1,0:T(2,128)(2,1)} %reshape.292), calls=%async_computation.5 | async-start | bytes 4718592 | tf_op jit(solution)/shard_map/all_to_all | solution.py:49
  427.2 20.3 %all-to-all-start.7 = ((f32[2,16,16]{2,0,1:T(2,128)}), f32[2,16,16]{2,0,1:T(2,128)S(1)}, u32[]{:S(2)}, u32[]{:S(2)}) async-start(f32[2,16,16]{2,0,1:T(2,128)} %copy.75), calls=%async_computation.7 | async-start | bytes 32768 | tf_op jit(solution)/shard_map/all_to_all | solution.py:48
  447.5 59.2 %all-to-all-start.6 = ((bf16[16,48,1536]{2,1,0:T(8,128)(2,1)}), bf16[16,48,1536]{2,1,0:T(8,128)(2,1)}, u32[]{:S(2)}, u32[]{:S(2)}) async-start(bf16[16,48,1536]{2,1,0:T(8,128)(2,1)} %broadcast_select_fusion), calls=%async_computation.6 | async-start | bytes 4718592 | tf_op jit(solution)/shard_map/all_to_all | solution.py:51
  506.6 3.4 copy-start.1
where the time goes:
time: 520 us; the launch traced here: 510 us
  local copies, waits for them, and re-layouts  198 us (38%)
  waiting for transfers between devices  136 us (26%)
  other arithmetic  83 us (16%)
  starting transfers between devices  39.8 us (8%)
  matrix products  34.8 us (7%)
  blocking collectives  18.4 us (4%)
    all_to_all x1, waiting for transfers between devices, local(): lax.all_to_all(chosen, 'walk', split_axis=0, concat_axis=1, tiled=True)  52.5 us
    all_to_all x1, waiting for transfers between devices, local(): lax.all_to_all(orbitals, 'walk', split_axis=1, concat_axis=0, tiled=True)  52.4 us
    reshape x4, local copies, waits for them, and re-layouts, local(): green = green.reshape(own_walkers, tile_rows, TILE, tile_rows, TILE)  48.1 us
    another operation x4, local copies, waits for them, and re-layouts  44.4 us
    unnamed x26, local copies, waits for them, and re-layouts  39.9 us
    convert_element_type x2, local copies, waits for them, and re-layouts, local(): dense.astype(jnp.bfloat16)  31.8 us
    unnamed x3, other arithmetic  24.1 us
    all_to_all x2, waiting for transfers between devices, local(): lax.all_to_all(picked, 'walk', split_axis=1, concat_axis=0, tiled=True)  21.4 us
  transfers between devices with their start and end apart: 7, of which 5 were waited for; matrix products, arithmetic and copies ran while one was open for 14% of the time, Pallas kernels for 0%

commit v1 on v0

v1 whole, which is shorter than its diff:
```python
import functools

import jax
import jax.numpy as jnp
from jax import lax
from jax.experimental import pallas as pl
from jax.experimental.pallas import tpu as pltpu
from jax.sharding import PartitionSpec as P

TILE = 64
LANES = 128
CHUNK = 256
VMEM_LIMIT = 52 * 1024 * 1024


def half_mask(rows):
    return lax.broadcasted_iota(jnp.int32, (rows, LANES), 1) < TILE


def pick_tile(green, row, col, odd):
    chunk = green[pl.ds(pl.multiple_of(row, TILE), TILE), pl.ds(pl.multiple_of(col, LANES), LANES)]
    chunk = chunk.astype(jnp.float32)
    low = lax.broadcasted_iota(jnp.int32, chunk.shape, 1) < TILE
    keep = low == (odd == 0)
    return jnp.where(keep, chunk, pltpu.roll(chunk, TILE, 1))


def add_tile(potential, row, col, odd, shift, block):
    total = shift[0:1] * block[0].astype(jnp.float32)
    for pair in range(1, len(block)):
        total = total + shift[pair : pair + 1] * block[pair].astype(jnp.float32)
    total = total + pltpu.roll(total, TILE, 1)
    total = (0.1 * total).astype(jnp.bfloat16).astype(jnp.float32)
    low = lax.broadcasted_iota(jnp.int32, total.shape, 1) < TILE
    keep = low == (odd == 0)
    at = (pl.ds(pl.multiple_of(row, TILE), TILE), pl.ds(pl.multiple_of(col, LANES), LANES))
    potential[at] = potential[at] + jnp.where(keep, total, 0.0)


def step_kernel(move, rows_ref, cols_ref, odds_ref, theta_t, orbitals, chol, fields, *rest):
    if move:
        bias_ref, shift_ref, out, green, potential = rest
    else:
        bias_ref, shift_ref, green = rest
    now = pl.program_id(0)
    blocks, pairs, slots = chol.shape[:3]
    width = orbitals.shape[1]

    @pl.when(now == 0)
    def _():
        @pl.loop(0, width // CHUNK)
        def _(i):
            at = pl.ds(pl.multiple_of(i * CHUNK, CHUNK), CHUNK)
            green[:, at] = jnp.dot(
                theta_t[...], orbitals[:, at], preferred_element_type=jnp.float32
            ).astype(green.dtype)
            if move:
                potential[:, at] = jnp.zeros((potential.shape[0], CHUNK), jnp.float32)

    @pl.loop(0, blocks)
    def _(b):
        base = (now * blocks + b) * slots
        acc = [jnp.zeros((8, LANES), jnp.float32) for _ in range(pairs)]
        for t in range(slots):
            g = pick_tile(green, rows_ref[base + t], cols_ref[base + t], odds_ref[base + t])
            for pair in range(pairs):
                product = g * chol[b, pair, t].astype(jnp.float32)
                acc[pair] = acc[pair] + jnp.sum(product.reshape(TILE // 8, 8, LANES), axis=0)
        sums = jnp.concatenate([jnp.sum(a, axis=0, keepdims=True) for a in acc], axis=0)
        low = half_mask(pairs)
        first = jnp.sum(jnp.where(low, sums, 0.0), axis=1, keepdims=True)
        second = jnp.sum(jnp.where(low, 0.0, sums), axis=1, keepdims=True)
        bias = jnp.where(low, first, second)
        shift = fields[b] - jnp.clip(0.5 * bias, -1.0, 1.0)
        bias_ref[b] = bias
        shift_ref[b] = shift
        if move:
            for t in range(slots):
                add_tile(
                    potential, rows_ref[base + t], cols_ref[base + t], odds_ref[base + t],
                    shift, [chol[b, pair, t] for pair in range(pairs)],
                )

    if move:
        @pl.when(now == pl.num_programs(0) - 1)
        def _():
            @pl.loop(0, width // CHUNK)
            def _(i):
                at = pl.ds(pl.multiple_of(i * CHUNK, CHUNK), CHUNK)
                moved = jnp.dot(
                    orbitals[...], potential[:, at].astype(jnp.bfloat16),
                    preferred_element_type=jnp.float32,
                )
                out[:, at] = (orbitals[:, at].astype(jnp.float32) + moved).astype(out.dtype)


def potential_kernel(rows_ref, cols_ref, odds_ref, chol, shifts, out1, out2, one, two):
    now = pl.program_id(0)
    blocks, pairs, slots = chol.shape[:3]
    width = one.shape[1]

    @pl.when(now == 0)
    def _():
        @pl.loop(0, width // CHUNK)
        def _(i):
            at = pl.ds(pl.multiple_of(i * CHUNK, CHUNK), CHUNK)
            one[:, at] = jnp.zeros((one.shape[0], CHUNK), jnp.float32)
            two[:, at] = jnp.zeros((two.shape[0], CHUNK), jnp.float32)

    @pl.loop(0, blocks)
    def _(b):
        base = (now * blocks + b) * slots
        for t in range(slots):
            block = [chol[b, pair, t] for pair in range(pairs)]
            place = (rows_ref[base + t], cols_ref[base + t], odds_ref[base + t])
            add_tile(one, *place, shifts[0, b], block)
            add_tile(two, *place, shifts[1, b], block)

    @pl.when(now == pl.num_programs(0) - 1)
    def _():
        @pl.loop(0, width // CHUNK)
        def _(i):
            at = pl.ds(pl.multiple_of(i * CHUNK, CHUNK), CHUNK)
            out1[:, at] = one[:, at].astype(out1.dtype)
            out2[:, at] = two[:, at].astype(out2.dtype)


def moves_kernel(orbitals, first, second, out, mid):
    width = orbitals.shape[1]

    def move(source, potential, target):
        @pl.loop(0, width // CHUNK)
        def _(i):
            at = pl.ds(pl.multiple_of(i * CHUNK, CHUNK), CHUNK)
            moved = jnp.dot(source[...], potential[:, at], preferred_element_type=jnp.float32)
            target[:, at] = (source[:, at].astype(jnp.float32) + moved).astype(target.dtype)

    move(orbitals, first, mid)
    move(mid, second, out)


def whole(shape):
    return pl.BlockSpec(shape, lambda i, *_: (0,) * len(shape), pipeline_mode=pl.Buffered(1))


def step(move, places, theta_t, orbitals, chol, fields):
    count, pairs, slots = chol.shape[:3]
    occupied, width = orbitals.shape
    per = 4 if count % 4 == 0 else 1
    lanes = pl.BlockSpec((per, pairs, LANES), lambda i, *_: (i, 0, 0))
    small = jax.ShapeDtypeStruct((count, pairs, LANES), jnp.float32)
    flops = 2 * occupied * width * width * (2 if move else 1)
    return pl.pallas_call(
        functools.partial(step_kernel, move),
        out_shape=(small, small) + ((jax.ShapeDtypeStruct((occupied, width), jnp.bfloat16),) if move else ()),
        grid_spec=pltpu.PrefetchScalarGridSpec(
            num_scalar_prefetch=3,
            grid=(count // per,),
            in_specs=[
                whole((width, occupied)),
                whole((occupied, width)),
                pl.BlockSpec((per, pairs, slots, TILE, LANES), lambda i, *_: (i, 0, 0, 0, 0)),
                lanes,
            ],
            out_specs=(lanes, lanes) + ((whole((occupied, width)),) if move else ()),
            scratch_shapes=[pltpu.VMEM((width, width), jnp.bfloat16)]
            + ([pltpu.VMEM((width, width), jnp.float32)] if move else []),
        ),
        compiler_params=pltpu.CompilerParams(vmem_limit_bytes=VMEM_LIMIT),
        cost_estimate=pl.CostEstimate(flops=flops, bytes_accessed=2 * chol.size, transcendentals=0),
        name="step",
    )(*places, theta_t, orbitals, chol, fields)


def potentials(places, chol, shifts, width):
    count, pairs, slots = chol.shape[:3]
    per = 4 if count % 4 == 0 else 1
    full = jax.ShapeDtypeStruct((width, width), jnp.bfloat16)
    return pl.pallas_call(
        potential_kernel,
        out_shape=(full, full),
        grid_spec=pltpu.PrefetchScalarGridSpec(
            num_scalar_prefetch=3,
            grid=(count // per,),
            in_specs=[
                pl.BlockSpec((per, pairs, slots, TILE, LANES), lambda i, *_: (i, 0, 0, 0, 0)),
                pl.BlockSpec((2, per, pairs, LANES), lambda i, *_: (0, i, 0, 0)),
            ],
            out_specs=(whole((width, width)),) * 2,
            scratch_shapes=[pltpu.VMEM((width, width), jnp.float32)] * 2,
        ),
        compiler_params=pltpu.CompilerParams(vmem_limit_bytes=VMEM_LIMIT),
        cost_estimate=pl.CostEstimate(flops=4 * chol.size, bytes_accessed=2 * chol.size, transcendentals=0),
        name="potentials",
    )(*places, chol, shifts)


def moves(orbitals, first, second):
    occupied, width = orbitals.shape
    vmem = pl.BlockSpec(memory_space=pltpu.VMEM)
    return pl.pallas_call(
        moves_kernel,
        out_shape=jax.ShapeDtypeStruct((occupied, width), jnp.bfloat16),
        in_specs=[vmem] * 3,
        out_specs=vmem,
        scratch_shapes=[pltpu.VMEM((occupied, width), jnp.bfloat16)],
        compiler_params=pltpu.CompilerParams(vmem_limit_bytes=VMEM_LIMIT),
        cost_estimate=pl.CostEstimate(
            flops=4 * occupied * width * width, bytes_accessed=4 * width * width, transcendentals=0
        ),
        name="moves",
    )(orbitals, first, second)


def spread(values, vectors):
    lead = values.shape[:-1]
    shaped = values.reshape(*lead, -1, vectors // 2, 2, 1)
    return jnp.broadcast_to(shaped, (*shaped.shape[:-1], TILE)).reshape(*shaped.shape[:-2], LANES)


def local(walkers, theta, cholesky, tiles, fields, source):
    own_walkers, occupied, width = walkers.shape
    tile_rows = width // TILE
    vectors, slots = cholesky.shape[1:3]

    halves = cholesky[0].astype(jnp.bfloat16).reshape(vectors // 2, 2, slots, TILE, TILE)
    halves = jnp.transpose(halves, (0, 2, 3, 1, 4)).reshape(vectors // 2, slots, TILE, LANES)
    chol = lax.all_gather(halves, "walk", axis=0, tiled=False)

    shares = lax.all_to_all(walkers, "walk", split_axis=1, concat_axis=0, tiled=True)
    chosen = jnp.take(shares, source, axis=0, mode="clip")
    origin = lax.all_to_all(chosen, "walk", split_axis=0, concat_axis=1, tiled=True)[0]

    flat = tiles.reshape(-1)
    row, col = flat // tile_rows, flat % tile_rows
    places = (row * TILE, (col // 2) * LANES, col % 2)
    theta_t = theta[0].T
    drive = spread(fields[:, 0], vectors)
    bias1, shift1, orbitals = step(True, places, theta_t, walkers[0], chol, drive[0])
    bias2, shift2 = step(False, places, theta_t, orbitals, chol, drive[1])
    biases = jnp.stack([bias1, bias2])[..., ::TILE].reshape(2, 1, -1)
    own_shift = jnp.stack([shift1, shift2])[..., ::TILE].reshape(2, -1)
    all_shifts = lax.all_gather(own_shift, "walk", axis=0, tiled=False)
    me = lax.axis_index("walk")
    mine = lax.dynamic_index_in_dim(source, me, 0, keepdims=False)
    chosen_shift = lax.dynamic_index_in_dim(all_shifts, mine, 0, keepdims=False)
    first, second = potentials(places, chol, spread(chosen_shift, vectors), width)
    return (moves(origin, first, second)[None], biases)


def solution(mesh):
    in_specs = (
        P(("groups", "walk"), None, None),
        P(("groups", "walk"), None, None),
        P(("groups", "walk"), None, None, None),
        P("groups", None),
        P(None, ("groups", "walk"), None),
        P("groups"),
    )
    out_specs = (P(("groups", "walk"), None, None), P(None, ("groups", "walk"), None))
    return jax.shard_map(local, mesh=mesh, in_specs=in_specs, out_specs=out_specs, check_vma=False)
```

time: 520 us -> 252 us (0.48); the launches traced: 510 us -> 248 us
  local copies, waits for them, and re-layouts: 198 us -> 32.8 us
  other arithmetic: 83 us -> 17.2 us
  Pallas kernels: 0 us -> 63.9 us
  waiting for transfers between devices: 136 us -> 86.7 us
  matrix products: 34.8 us -> 0 us
  starting transfers between devices: 39.8 us -> 11.7 us
  between operations: 1.34 us -> 16.2 us
    pallas_call x0 -> x4, Pallas kernels: none -> 63.9 us  [the longest x2 35.3 us: step(): pl.pallas_call(functools.partial(step_kernel, move), out_shape=(small, sm...]
    all_to_all x7 -> x2, waiting for transfers between devices: 136 us -> 86.7 us  [the longest x1 86.7 us: local(): lax.all_to_all(walkers, 'walk', split_axis=1, concat_axis=0, tiled=True)]
    reshape x4 -> x2, local copies, waits for them, and re-layouts: 48.1 us -> 0.91 us  [the longest x1 0.72 us: local(): biases = jnp.stack([bias1, bias2])[..., ::TILE].reshape(2, 1, -1)]
    another operation x7 -> x2, local copies, waits for them, and re-layouts: 48.2 us -> 1.44 us  [the longest x1 1.31 us: local(): chol = lax.all_gather(halves, 'walk', axis=0, tiled=False)]
    convert_element_type x5 -> x2, local copies, waits for them, and re-layouts: 44.6 us -> 1.88 us  [local(): cholesky[0].astype(jnp.bfloat16).reshape(vectors // 2, 2, slots, TILE, TILE)]
    dot_general x8 -> x0, matrix products: 34.8 us -> none  [the longest x2 15.3 us: local(): jnp.einsum('wik,wkl->wil', orbitals, potential, preferred_element_type=jn...]
    all_to_all x7 -> x2, starting transfers between devices: 39.8 us -> 11.7 us  [the longest x1 6.69 us: local(): lax.all_to_all(walkers, 'walk', split_axis=1, concat_axis=0, tiled=True)]
    convert_element_type x4 -> x1, other arithmetic: 29.3 us -> 1.44 us  [local(): cholesky[0].astype(jnp.bfloat16).reshape(vectors // 2, 2, slots, TILE, TILE)]
  transfers between devices with their start and end apart: 7 -> 3, of which waited for: 5 -> 1; matrix products, arithmetic and copies ran while one was open for 14% -> 18% of each run, Pallas kernels for 0% -> 20%
where the time goes in v1:
time: 252 us; the launch traced here: 248 us
  waiting for transfers between devices  86.7 us (34%)
  Pallas kernels  63.9 us (25%)
  local copies, waits for them, and re-layouts  32.8 us (13%)
  blocking collectives  19.2 us (8%)
  other arithmetic  17.2 us (7%)
  between operations  16.2 us (6%)
  starting transfers between devices  11.7 us (5%)
    all_to_all x1, waiting for transfers between devices, local(): lax.all_to_all(walkers, 'walk', split_axis=1, concat_axis=0, tiled=True)  86.7 us
    pallas_call x2, Pallas kernels, step(): pl.pallas_call(functools.partial(step_kernel, move), out_shape=(small, sm...  35.3 us
    unnamed x14, local copies, waits for them, and re-layouts  23.4 us
    all_gather x1, blocking collectives, local(): all_shifts = lax.all_gather(own_shift, 'walk', axis=0, tiled=False)  19.2 us
    unnamed x1, other arithmetic  15.7 us
    pallas_call x1, Pallas kernels, moves(): pl.pallas_call(moves_kernel, out_shape=jax.ShapeDtypeStruct((occupied, wi...  15.3 us
    pallas_call x1, Pallas kernels, potentials(): pl.pallas_call(potential_kernel, out_shape=(full, full), grid_spec=pltpu....  13.3 us
    all_to_all x1, starting transfers between devices, local(): lax.all_to_all(walkers, 'walk', split_axis=1, concat_axis=0, tiled=True)  6.69 us
  transfers between devices with their start and end apart: 3, of which 1 were waited for; matrix products, arithmetic and copies ran while one was open for 18% of the time, Pallas kernels for 20%

profile of v1, /device:TPU:13, one launch (start us, length us, event | category | flops | bytes accessed | tf_op | source)
XLA Modules:
  0.0 247.7 jit_solution(16029705472201751536)
XLA Ops:
  7.2 1.4 convert_element_type.7
  8.7 0.8 convert_element_type.8
  9.5 1.1 copy.37
  10.6 1.3 all_gather_reshape.6
  11.9 7.5 %copy.38 = bf16[1,768,1536]{2,0,1:T(2,128)(2,1)} copy(bf16[1,768,1536]{2,1,0:T(8,128)(2,1)} %param.6) | data formatting | bytes 4718592 | tf_op args[0]
  19.4 0.5 broadcast.32
  19.9 15.7 %reduce.8 = bf16[768,1536]{1,0:T(8,128)(2,1)S(1)} reduce(bf16[768,1,1536]{2,1,0:T(2,128)(2,1)} %bitcast.27, bf16[]{:T(256)} %broadcast.32), dimensions={1}, to_apply=%bitcast.22.reduce_sub_computation | reduce | bytes 4718594
  35.6 3.0 %reshape.69 = bf16[16,2,36864]{2,1,0:T(2,128)(2,1)} reshape(bf16[768,1536]{1,0:T(8,128)(2,1)S(1)} %reduce.8) | data formatting | bytes 4718592
  38.6 6.7 %all-to-all-start = ((bf16[16,2,36864]{2,1,0:T(2,128)(2,1)}), bf16[16,2,36864]{2,1,0:T(2,128)(2,1)S(1)}, u32[]{:S(2)}, u32[]{:S(2)}) async-start(bf16[16,2,36864]{2,1,0:T(2,128)(2,1)} %reshape.69), calls=%async_computation | async-start | bytes 4718592 | tf_op jit(solution)/shard_map/all_to_all | solution.py:230
  45.3 86.7 %all-to-all-done = bf16[16,2,36864]{2,1,0:T(2,128)(2,1)S(1)} async-done(((bf16[16,2,36864]{2,1,0:T(2,128)(2,1)}), bf16[16,2,36864]{2,1,0:T(2,128)(2,1)S(1)}, u32[]{:S(2)}, u32[]{:S(2)}) %all-to-all-start) | async-done | bytes 2359328 | tf_op jit(solution)/shard_map/all_to_all | solution.py:230
  131.9 7.0 %reshape.70 = bf16[768,1,1536]{2,1,0:T(2,128)(2,1)} reshape(bf16[16,2,36864]{2,1,0:T(2,128)(2,1)S(1)} %all-to-all-done) | data formatting | bytes 4718592
  138.9 2.9 %copy.34 = bf16[1,768,1536]{2,1,0:T(8,128)(2,1)S(1)} copy(bf16[1,768,1536]{2,0,1:T(2,128)(2,1)} %bitcast.28) | data formatting | bytes 4718592
  141.9 2.1 gather_fusion
  144.0 5.0 %all-to-all-start.1 = ((bf16[16,48,1536]{2,1,0:T(8,128)(2,1)}), bf16[16,48,1536]{2,1,0:T(8,128)(2,1)}, u32[]{:S(2)}, u32[]{:S(2)}) async-start(bf16[16,48,1536]{2,1,0:T(8,128)(2,1)} %gather_fusion), calls=%async_computation.1 | async-start | bytes 4718592 | tf_op jit(solution)/shard_map/all_to_all | solution.py:232
  149.0 0.6 dynamic_slice.8
  152.4 2.5 %copy.32 = bf16[1,768,1536]{1,2,0:T(8,128)(2,1)} copy(bf16[1,768,1536]{2,1,0:T(8,128)(2,1)S(1)} %copy-done) | data formatting | bytes 4718592 | tf_op args[1]
  155.6 22.0 %step.2 = (f32[16,8,128]{2,1,0:T(8,128)S(1)}, f32[16,8,128]{2,1,0:T(8,128)S(1)}, bf16[768,1536]{1,0:T(8,128)(2,1)}) custom-call(s32[64]{0:T(128)S(1)} %get-tuple-element.31.rows_ref, s32[64]{0:T(128)S(1)} %get-tuple-element.30.cols_ref, s32[64]{0:T(128)S(1)} %get-tuple-element.26.odds_ref, bf16[1536,768]{1,0:T(8,128)(2,1)} %bitcast.32, ...), custom_call_target="tpu_custom_call" | custom-call | flops 7247757312 | bytes 8388608 | tf_op jit(solution)/shard_map/step/pallas_call | solution.py:153
  177.7 13.3 %step.3 = (f32[16,8,128]{2,1,0:T(8,128)S(1)}, f32[16,8,128]{2,1,0:T(8,128)S(1)}) custom-call(s32[64]{0:T(128)S(1)} %get-tuple-element.31.rows_ref, s32[64]{0:T(128)S(1)} %get-tuple-element.30.cols_ref, s32[64]{0:T(128)S(1)} %get-tuple-element.26.odds_ref, bf16[1536,768]{1,0:T(8,128)(2,1)} %bitcast.33, bf16[768,1536]{1,0:T(8,128)(2,1)} %get-tuple-element.10.orbitals, ...), custom_call_target="tpu_custom_call" | custom-call | flops 3623878656 | bytes 8388608 | tf_op jit(solution)/shard_map/step/pallas_call | solution.py:153
  191.0 0.2 slice.26
  191.6 0.7 reshape.56
  192.3 19.2 %all_gather.7 = f32[16,2,256]{2,1,0:T(2,128)S(1)} all-gather(f32[1,2,256]{2,1,0:T(2,128)S(1)} %all_gather_reshape.7), channel_id=1, replica_groups=mesh['groups'=2,'walk'=16] {'walk'}, dimensions={0}, use_global_device_ids=true | all-gather | bytes 34816 | tf_op jit(solution)/shard_map/all_gather | solution.py:243
  211.7 0.3 broadcast_in_dim.31
  212.2 13.3 %potentials.1 = (bf16[1536,1536]{1,0:T(8,128)(2,1)}, bf16[1536,1536]{1,0:T(8,128)(2,1)}) custom-call(s32[64]{0:T(128)S(1)} %get-tuple-element.31.rows_ref, s32[64]{0:T(128)S(1)} %get-tuple-element.30.cols_ref, s32[64]{0:T(128)S(1)} %get-tuple-element.26.odds_ref, bf16[16,8,4,64,128]{4,3,2,1,0:T(8,128)(2,1)} %all-gather.2.cloned.1.call-done.chol, ...), custom_call_target="tpu_custom_call" | custom-call | flops 16777216 | bytes 8388608 | tf_op jit(solution)/shard_map/potentials/pallas_call | solution.py:179
  225.5 15.3 %moves.1 = bf16[768,1536]{1,0:T(8,128)(2,1)} custom-call(bf16[768,1536]{1,0:T(8,128)(2,1)} %bitcast.orbitals, bf16[1536,1536]{1,0:T(8,128)(2,1)} %get-tuple-element.12.first, bf16[1536,1536]{1,0:T(8,128)(2,1)} %get-tuple-element.13.second), custom_call_target="tpu_custom_call" | custom-call | flops 7247757312 | bytes 9437184 | tf_op jit(solution)/shard_map/moves/pallas_call | solution.py:201
  (37 shorter events, 2.4 us)
Async XLA Ops:
  7.2 148.5 %all-gather.2.cloned.1.call-start = ((), (), s32[]{:S(2)}) async-start(), calls=%async_computation.2 | async-start | bytes 8912896 | tf_op jit(solution)/shard_map/all_gather | solution.py:228
  38.5 6.7 %copy-start.3 = (s32[16]{0:T(128)S(1)}, s32[16]{0:T(128)}, u32[]{:S(2)}) copy-start(s32[16]{0:T(128)} %param.11) | copy-start | bytes 196
  38.6 93.4 %all-to-all-start = ((bf16[16,2,36864]{2,1,0:T(2,128)(2,1)}), bf16[16,2,36864]{2,1,0:T(2,128)(2,1)S(1)}, u32[]{:S(2)}, u32[]{:S(2)}) async-start(bf16[16,2,36864]{2,1,0:T(2,128)(2,1)} %reshape.69), calls=%async_computation | async-start | bytes 4718592 | tf_op jit(solution)/shard_map/all_to_all | solution.py:230
  144.0 6.9 %copy-start.1 = (s32[16,4]{0,1:T(4,128)S(1)}, s32[16,4]{0,1:T(4,128)}, u32[]{:S(2)}) copy-start(s32[16,4]{0,1:T(4,128)} %param.9) | copy-start | bytes 772
  144.0 7.5 %copy-start.2 = (f32[2,1,256]{2,1,0:T(1,128)S(1)}, f32[2,1,256]{2,1,0:T(1,128)}, u32[]{:S(2)}) copy-start(f32[2,1,256]{2,1,0:T(1,128)} %param.10) | copy-start | bytes 6148
  144.0 8.4 %copy-start = (bf16[1,768,1536]{2,1,0:T(8,128)(2,1)S(1)}, bf16[1,768,1536]{2,1,0:T(8,128)(2,1)}, u32[]{:S(2)}) copy-start(bf16[1,768,1536]{2,1,0:T(8,128)(2,1)} %param.7) | copy-start | bytes 7077892
  144.0 81.6 %all-to-all-start.1 = ((bf16[16,48,1536]{2,1,0:T(8,128)(2,1)}), bf16[16,48,1536]{2,1,0:T(8,128)(2,1)}, u32[]{:S(2)}, u32[]{:S(2)}) async-start(bf16[16,48,1536]{2,1,0:T(8,128)(2,1)} %gather_fusion), calls=%async_computation.1 | async-start | bytes 4718592 | tf_op jit(solution)/shard_map/all_to_all | solution.py:232
Sparse Core Ops, SparseCore 0:
  12.0 111.0 all-gather.1

commit v2 on v1

--- a/solution.py
+++ b/solution.py
@@ -7,10 +7,185 @@
 from jax.experimental.pallas import tpu as pltpu
 from jax.sharding import PartitionSpec as P
 
+MESH = pl.DeviceIdType.MESH
 TILE = 64
 LANES = 128
 CHUNK = 256
 VMEM_LIMIT = 52 * 1024 * 1024
+
+
+def plane(count):
+    chips = count // 2
+    short = 1
+    while (2 * short) * (2 * short) <= chips and chips % (2 * short) == 0:
+        short *= 2
+    return chips // short, short
+
+
+def greet(count, me):
+    barrier = pltpu.get_barrier_semaphore()
+
+    @pl.loop(1, count)
+    def _(k):
+        pl.semaphore_signal(
+            barrier, inc=1, device_id={"walk": lax.rem(me + k, count)}, device_id_type=MESH
+        )
+
+    pl.semaphore_wait(barrier, count - 1)
+
+
+def exchange_kernel(count, own, rows, blocks, shares, own_sem, send, recv, row_send, row_recv):
+    long, short = plane(count)
+    me = lax.axis_index("walk")
+    core = lax.rem(me, 2)
+    y = lax.rem(me // 2, short)
+    z = me // (2 * short)
+
+    def index(a, b, c):
+        return (a * short + b) * 2 + c
+
+    def hop(source, slot, way, target):
+        return pltpu.make_async_remote_copy(
+            src_ref=source, dst_ref=blocks.at[slot], send_sem=send.at[way, slot],
+            recv_sem=recv.at[slot], device_id={"walk": target}, device_id_type=MESH,
+        )
+
+    def row_copy(k):
+        target = lax.rem(me + k, count)
+        return pltpu.make_async_remote_copy(
+            src_ref=rows.at[target], dst_ref=shares.at[me], send_sem=row_send.at[k],
+            recv_sem=row_recv.at[k], device_id={"walk": target}, device_id_type=MESH,
+        )
+
+    def ways(dz, dy):
+        line = dy == 0
+        return (
+            (0, line & (dz <= 0) & (z < long - 1), index(z + 1, y, core)),
+            (1, line & (dz >= 0) & (z > 0), index(z - 1, y, core)),
+            (2, (dy <= 0) & (y < short - 1), index(z, y + 1, core)),
+            (3, (dy >= 0) & (y > 0), index(z, y - 1, core)),
+        )
+
+    def signed(k):
+        return jnp.where(lax.rem(k, 2) == 1, (k + 1) // 2, -(k // 2))
+
+    spread_z, spread_y = 2 * long - 1, 2 * short - 1
+    greet(count, me)
+
+    for way, whether, target in ways(0, 0):
+        @pl.when(whether)
+        def _(way=way, target=target):
+            hop(own, me, way, target).start()
+    hop(own, me, 4, index(z, y, 1 - core)).start()
+
+    @pl.loop(1, count)
+    def _(k):
+        row_copy(k).start()
+
+    keep = pltpu.make_async_copy(own, blocks.at[me], own_sem.at[0])
+    keep_rows = pltpu.make_async_copy(rows.at[me], shares.at[me], own_sem.at[1])
+    keep.start()
+    keep_rows.start()
+
+    def each(act, start):
+        @pl.loop(start, spread_z * spread_y)
+        def _(k):
+            dy, dz = signed(k // spread_z), signed(lax.rem(k, spread_z))
+            inside = (z + dz >= 0) & (z + dz < long) & (y + dy >= 0) & (y + dy < short)
+
+            @pl.when(inside)
+            def _():
+                act(dz, dy, index(z + dz, y + dy, core))
+
+    def forward(dz, dy, slot):
+        hop(own, slot, 0, index(z, y, 1 - core)).wait_recv()
+        for way, whether, target in ways(dz, dy):
+            @pl.when(whether)
+            def _(way=way, target=target):
+                hop(blocks.at[slot], slot, way, target).start()
+        hop(blocks.at[slot], slot, 4, index(z, y, 1 - core)).start()
+
+    def finish(dz, dy, slot):
+        for way, whether, target in ways(dz, dy):
+            @pl.when(whether)
+            def _(way=way, target=target):
+                hop(own, slot, way, target).wait_send()
+        hop(own, slot, 4, index(z, y, 1 - core)).wait_send()
+        other = slot + 1 - 2 * core
+        hop(own, other, 4, index(z, y, 1 - core)).wait_recv()
+
+    each(forward, 1)
+    each(finish, 0)
+    keep.wait()
+    keep_rows.wait()
+
+    @pl.loop(1, count)
+    def _(k):
+        row_copy(k).wait()
+
+
+def exchange(own, rows):
+    count = rows.shape[0]
+    anywhere = pl.BlockSpec(memory_space=pl.ANY)
+    return pl.pallas_call(
+        functools.partial(exchange_kernel, count),
+        out_shape=(
+            jax.ShapeDtypeStruct((count, *own.shape), own.dtype),
+            jax.ShapeDtypeStruct(rows.shape, rows.dtype),
+        ),
+        in_specs=[anywhere] * 2,
+        out_specs=(anywhere,) * 2,
+        scratch_shapes=[
+            pltpu.SemaphoreType.DMA((2,)),
+            pltpu.SemaphoreType.DMA((5, count)),
+            pltpu.SemaphoreType.DMA((count,)),
+            pltpu.SemaphoreType.DMA((count,)),
+            pltpu.SemaphoreType.DMA((count,)),
+        ],
+        compiler_params=pltpu.CompilerParams(collective_id=0, has_side_effects=True),
+        name="exchange",
+    )(own, rows)
+
+
+def shifts_kernel(count, own, every, own_sem, send, recv):
+    me = lax.axis_index("walk")
+
+    def copy(k):
+        return pltpu.make_async_remote_copy(
+            src_ref=own, dst_ref=every.at[me], send_sem=send.at[k], recv_sem=recv.at[k],
+            device_id={"walk": lax.rem(me + k, count)}, device_id_type=MESH,
+        )
+
+    greet(count, me)
+
+    @pl.loop(1, count)
+    def _(k):
+        copy(k).start()
+
+    keep = pltpu.make_async_copy(own, every.at[me], own_sem)
+    keep.start()
+    keep.wait()
+
+    @pl.loop(1, count)
+    def _(k):
+        copy(k).wait()
+
+
+def gather_shifts(own, count):
+    vmem = pl.BlockSpec(memory_space=pltpu.VMEM)
+    return pl.pallas_call(
+        functools.partial(shifts_kernel, count),
+        out_shape=jax.ShapeDtypeStruct((count, *own.shape), own.dtype),
+        in_specs=[vmem],
+        out_specs=vmem,
+        scratch_shapes=[
+            pltpu.SemaphoreType.DMA,
+            pltpu.SemaphoreType.DMA((count,)),
+            pltpu.SemaphoreType.DMA((count,)),
+        ],
+        compiler_params=pltpu.CompilerParams(collective_id=1, has_side_effects=True),
+        name="gather_shifts",
+    )(own)
 
 
 def half_mask(rows):
@@ -39,9 +214,9 @@
 
 def step_kernel(move, rows_ref, cols_ref, odds_ref, theta_t, orbitals, chol, fields, *rest):
     if move:
-        bias_ref, shift_ref, out, green, potential = rest
+        bias_ref, shift_ref, out, green, sums, potential = rest
     else:
-        bias_ref, shift_ref, green = rest
+        bias_ref, shift_ref, green, sums = rest
     now = pl.program_id(0)
     blocks, pairs, slots = chol.shape[:3]
     width = orbitals.shape[1]
@@ -57,8 +232,7 @@
             if move:
                 potential[:, at] = jnp.zeros((potential.shape[0], CHUNK), jnp.float32)
 
-    @pl.loop(0, blocks)
-    def _(b):
+    for b in range(blocks):
         base = (now * blocks + b) * slots
         acc = [jnp.zeros((8, LANES), jnp.float32) for _ in range(pairs)]
         for t in range(slots):
@@ -66,15 +240,19 @@
             for pair in range(pairs):
                 product = g * chol[b, pair, t].astype(jnp.float32)
                 acc[pair] = acc[pair] + jnp.sum(product.reshape(TILE // 8, 8, LANES), axis=0)
-        sums = jnp.concatenate([jnp.sum(a, axis=0, keepdims=True) for a in acc], axis=0)
-        low = half_mask(pairs)
-        first = jnp.sum(jnp.where(low, sums, 0.0), axis=1, keepdims=True)
-        second = jnp.sum(jnp.where(low, 0.0, sums), axis=1, keepdims=True)
-        bias = jnp.where(low, first, second)
-        shift = fields[b] - jnp.clip(0.5 * bias, -1.0, 1.0)
-        bias_ref[b] = bias
-        shift_ref[b] = shift
-        if move:
+        for pair in range(pairs):
+            sums[b, pair] = acc[pair]
+    rows = jnp.sum(sums[...], axis=2).reshape(blocks * pairs, LANES)
+    low = half_mask(blocks * pairs)
+    first = jnp.sum(jnp.where(low, rows, 0.0), axis=1, keepdims=True)
+    second = jnp.sum(jnp.where(low, 0.0, rows), axis=1, keepdims=True)
+    bias = jnp.where(low, first, second).reshape(blocks, pairs, LANES)
+    bias_ref[...] = bias
+    shift_ref[...] = fields[...] - jnp.clip(0.5 * bias, -1.0, 1.0)
+    if move:
+        for b in range(blocks):
+            base = (now * blocks + b) * slots
+            shift = shift_ref[b]
             for t in range(slots):
                 add_tile(
                     potential, rows_ref[base + t], cols_ref[base + t], odds_ref[base + t],
@@ -163,7 +341,10 @@
                 lanes,
             ],
             out_specs=(lanes, lanes) + ((whole((occupied, width)),) if move else ()),
-            scratch_shapes=[pltpu.VMEM((width, width), jnp.bfloat16)]
+            scratch_shapes=[
+                pltpu.VMEM((width, width), jnp.bfloat16),
+                pltpu.VMEM((per, pairs, 8, LANES), jnp.float32),
+            ]
             + ([pltpu.VMEM((width, width), jnp.float32)] if move else []),
         ),
         compiler_params=pltpu.CompilerParams(vmem_limit_bytes=VMEM_LIMIT),
@@ -225,11 +406,11 @@
 
     halves = cholesky[0].astype(jnp.bfloat16).reshape(vectors // 2, 2, slots, TILE, TILE)
     halves = jnp.transpose(halves, (0, 2, 3, 1, 4)).reshape(vectors // 2, slots, TILE, LANES)
-    chol = lax.all_gather(halves, "walk", axis=0, tiled=False)
-
-    shares = lax.all_to_all(walkers, "walk", split_axis=1, concat_axis=0, tiled=True)
+    count = source.shape[0]
+    chol, shares = exchange(halves, walkers.reshape(count, occupied // count, width))
     chosen = jnp.take(shares, source, axis=0, mode="clip")
-    origin = lax.all_to_all(chosen, "walk", split_axis=0, concat_axis=1, tiled=True)[0]
+    origin = lax.all_to_all(chosen, "walk", split_axis=0, concat_axis=0, tiled=True)
+    origin = origin.reshape(occupied, width)
 
     flat = tiles.reshape(-1)
     row, col = flat // tile_rows, flat % tile_rows
@@ -240,7 +421,7 @@
     bias2, shift2 = step(False, places, theta_t, orbitals, chol, drive[1])
     biases = jnp.stack([bias1, bias2])[..., ::TILE].reshape(2, 1, -1)
     own_shift = jnp.stack([shift1, shift2])[..., ::TILE].reshape(2, -1)
-    all_shifts = lax.all_gather(own_shift, "walk", axis=0, tiled=False)
+    all_shifts = gather_shifts(own_shift, count)
     me = lax.axis_index("walk")
     mine = lax.dynamic_index_in_dim(source, me, 0, keepdims=False)
     chosen_shift = lax.dynamic_index_in_dim(all_shifts, mine, 0, keepdims=False)

time: 252 us -> 211 us (0.84)
  Pallas kernels: 63.9 us -> 170 us
  waiting for transfers between devices: 86.7 us -> 0.01 us
  blocking collectives: 19.2 us -> 0 us
  local copies, waits for them, and re-layouts: 32.8 us -> 14.9 us
  other arithmetic: 17.2 us -> 2.18 us
  between operations: 16.2 us -> 2.7 us
  starting transfers between devices: 11.7 us -> 17.9 us
    pallas_call x0 -> x2, Pallas kernels: none -> 110 us  [the longest x1 94.8 us: exchange(): pl.pallas_call(functools.partial(exchange_kernel, count), out_shape=(jax....]
    all_to_all x2 -> x1, waiting for transfers between devices: 86.7 us -> 0.01 us  [local(): lax.all_to_all(chosen, 'walk', split_axis=0, concat_axis=0, tiled=True)]
    unnamed x14 -> x9, local copies, waits for them, and re-layouts: 23.4 us -> 2.54 us
    all_gather x1 -> x0, blocking collectives: 19.2 us -> none  [local(): all_shifts = lax.all_gather(own_shift, 'walk', axis=0, tiled=False)]
    unnamed x1 -> x0, other arithmetic: 15.7 us -> none
    all_to_all x2 -> x1, starting transfers between devices: 11.7 us -> 17.9 us  [local(): lax.all_to_all(chosen, 'walk', split_axis=0, concat_axis=0, tiled=True)]
    pallas_call x2, Pallas kernels: 35.3 us -> 31.8 us  [step(): pl.pallas_call(functools.partial(step_kernel, move), out_shape=(small, sm...]
  transfers between devices with their start and end apart: 3 -> 1, of which waited for: 1 -> 0; matrix products, arithmetic and copies ran while one was open for 18% -> 4% of each run, Pallas kernels for 20% -> 29%
where the time goes in v2:
time: 211 us; the launch traced here: 208 us
  Pallas kernels  170 us (81%)
  starting transfers between devices  17.9 us (8%)
  local copies, waits for them, and re-layouts  14.9 us (7%)
  between operations  2.7 us (1%)
  other arithmetic  2.18 us (1%)
    pallas_call x1, Pallas kernels, exchange(): pl.pallas_call(functools.partial(exchange_kernel, count), out_shape=(jax....  94.8 us
    pallas_call x2, Pallas kernels, step(): pl.pallas_call(functools.partial(step_kernel, move), out_shape=(small, sm...  31.8 us
    all_to_all x1, starting transfers between devices, local(): lax.all_to_all(chosen, 'walk', split_axis=0, concat_axis=0, tiled=True)  17.9 us
    pallas_call x1, Pallas kernels, moves(): pl.pallas_call(moves_kernel, out_shape=jax.ShapeDtypeStruct((occupied, wi...  15.3 us
    pallas_call x1, Pallas kernels, gather_shifts(): pl.pallas_call(functools.partial(shifts_kernel, count), out_shape=jax.Sha...  15.1 us
    pallas_call x1, Pallas kernels, potentials(): pl.pallas_call(potential_kernel, out_shape=(full, full), grid_spec=pltpu....  13.3 us
  transfers between devices with their start and end apart: 1, of which 0 were waited for; matrix products, arithmetic and copies ran while one was open for 4% of the time, Pallas kernels for 29%

profile of v2, /device:TPU:13, one launch (start us, length us, event | category | flops | bytes accessed | tf_op | source)
XLA Modules:
  0.0 207.9 jit_solution(10542051342402409328)
XLA Ops:
  0.6 0.7 pad_clamp_fusion
  1.3 1.4 convert_element_type.7
  2.7 0.8 convert_element_type.8
  3.5 1.1 copy.21
  4.6 1.3 reshape.50.own
  5.9 94.8 %exchange.1 = (bf16[16,8,4,64,128]{4,3,2,1,0:T(8,128)(2,1)}, bf16[16,48,1536]{2,1,0:T(8,128)(2,1)}) custom-call(bf16[8,4,64,128]{3,2,1,0:T(8,128)(2,1)} %reshape.50.own, bf16[16,48,1536]{2,1,0:T(8,128)(2,1)} %bitcast.24), custom_call_target="tpu_custom_call" | custom-call | tf_op jit(solution)/shard_map/exchange/pallas_call | solution.py:130
  100.8 3.8 %gather_fusion = bf16[16,48,1536]{2,1,0:T(8,128)(2,1)} fusion(bf16[16,48,1536]{2,1,0:T(8,128)(2,1)} %get-tuple-element.11, s32[1024]{0:T(1024)S(1)} %pad_clamp_fusion), kind=kCustom, calls=%fused_computation | custom fusion | bytes 4718656 | tf_op jit(solution)/shard_map/jit(_take)/gather | solution.py:411
  104.6 17.9 %all-to-all-start = ((bf16[16,48,1536]{2,1,0:T(8,128)(2,1)}), bf16[16,48,1536]{2,1,0:T(8,128)(2,1)}, u32[]{:S(2)}, u32[]{:S(2)}) async-start(bf16[16,48,1536]{2,1,0:T(8,128)(2,1)} %gather_fusion), calls=%async_computation | async-start | bytes 4718592 | tf_op jit(solution)/shard_map/all_to_all | solution.py:412
  122.4 0.6 dynamic_slice.8
  125.1 0.2 broadcast_in_dim.28
  125.5 0.2 broadcast_in_dim.26
  125.9 2.5 %copy.18 = bf16[1,768,1536]{1,2,0:T(8,128)(2,1)} copy(bf16[1,768,1536]{2,1,0:T(8,128)(2,1)S(1)} %copy-done) | data formatting | bytes 4718592 | tf_op args[1]
  128.4 19.8 %step.2 = (f32[16,8,128]{2,1,0:T(8,128)S(1)}, f32[16,8,128]{2,1,0:T(8,128)S(1)}, bf16[768,1536]{1,0:T(8,128)(2,1)}) custom-call(s32[64]{0:T(128)S(1)} %get-tuple-element.31.rows_ref, s32[64]{0:T(128)S(1)} %get-tuple-element.30.cols_ref, s32[64]{0:T(128)S(1)} %get-tuple-element.26.odds_ref, bf16[1536,768]{1,0:T(8,128)(2,1)} %bitcast.26, ...), custom_call_target="tpu_custom_call" | custom-call | flops 7247757312 | bytes 8388608 | tf_op jit(solution)/shard_map/step/pallas_call | solution.py:331
  148.2 12.0 %step.3 = (f32[16,8,128]{2,1,0:T(8,128)S(1)}, f32[16,8,128]{2,1,0:T(8,128)S(1)}) custom-call(s32[64]{0:T(128)S(1)} %get-tuple-element.31.rows_ref, s32[64]{0:T(128)S(1)} %get-tuple-element.30.cols_ref, s32[64]{0:T(128)S(1)} %get-tuple-element.26.odds_ref, bf16[1536,768]{1,0:T(8,128)(2,1)} %bitcast.27, bf16[768,1536]{1,0:T(8,128)(2,1)} %get-tuple-element.14.orbitals, ...), custom_call_target="tpu_custom_call" | custom-call | flops 3623878656 | bytes 8388608 | tf_op jit(solution)/shard_map/step/pallas_call | solution.py:331
  160.3 0.2 slice.26
  160.5 0.7 reshape.53.own
  161.3 0.2 slice.27
  161.5 0.7 reshape.65
  162.2 15.1 %gather_shifts.1 = f32[16,2,256]{2,1,0:T(2,128)} custom-call(f32[2,256]{1,0:T(2,128)} %reshape.53.own), custom_call_target="tpu_custom_call" | custom-call | tf_op jit(solution)/shard_map/gather_shifts/pallas_call | solution.py:176
  178.0 0.7 constant_dynamic-slice_fusion
  178.8 0.3 broadcast_in_dim.31
  179.1 0.2 reshape.54.shifts
  179.3 13.3 %potentials.1 = (bf16[1536,1536]{1,0:T(8,128)(2,1)}, bf16[1536,1536]{1,0:T(8,128)(2,1)}) custom-call(s32[64]{0:T(128)S(1)} %get-tuple-element.31.rows_ref, s32[64]{0:T(128)S(1)} %get-tuple-element.30.cols_ref, s32[64]{0:T(128)S(1)} %get-tuple-element.26.odds_ref, bf16[16,8,4,64,128]{4,3,2,1,0:T(8,128)(2,1)} %get-tuple-element.12.chol, ...), custom_call_target="tpu_custom_call" | custom-call | flops 16777216 | bytes 8388608 | tf_op jit(solution)/shard_map/potentials/pallas_call | solution.py:360
  192.6 15.3 %moves.1 = bf16[768,1536]{1,0:T(8,128)(2,1)} custom-call(bf16[768,1536]{1,0:T(8,128)(2,1)} %bitcast.2.orbitals, bf16[1536,1536]{1,0:T(8,128)(2,1)} %get-tuple-element.16.first, bf16[1536,1536]{1,0:T(8,128)(2,1)} %get-tuple-element.17.second), custom_call_target="tpu_custom_call" | custom-call | flops 7247757312 | bytes 9437184 | tf_op jit(solution)/shard_map/moves/pallas_call | solution.py:382
  (27 shorter events, 1.3 us)
Async XLA Ops:
  104.5 17.9 %copy-start.3 = (s32[16]{0:T(128)S(1)}, s32[16]{0:T(128)}, u32[]{:S(2)}) copy-start(s32[16]{0:T(128)} %param.11) | copy-start | bytes 196
  104.5 19.8 %copy-start.1 = (s32[16,4]{0,1:T(4,128)S(1)}, s32[16,4]{0,1:T(4,128)}, u32[]{:S(2)}) copy-start(s32[16,4]{0,1:T(4,128)} %param.9) | copy-start | bytes 772
  104.5 20.3 %copy-start.2 = (f32[2,1,256]{2,1,0:T(1,128)S(1)}, f32[2,1,256]{2,1,0:T(1,128)}, u32[]{:S(2)}) copy-start(f32[2,1,256]{2,1,0:T(1,128)} %param.10) | copy-start | bytes 6148
  104.5 21.3 %copy-start = (bf16[1,768,1536]{2,1,0:T(8,128)(2,1)S(1)}, bf16[1,768,1536]{2,1,0:T(8,128)(2,1)}, u32[]{:S(2)}) copy-start(bf16[1,768,1536]{2,1,0:T(8,128)(2,1)} %param.7) | copy-start | bytes 7077892
  104.6 88.1 %all-to-all-start = ((bf16[16,48,1536]{2,1,0:T(8,128)(2,1)}), bf16[16,48,1536]{2,1,0:T(8,128)(2,1)}, u32[]{:S(2)}, u32[]{:S(2)}) async-start(bf16[16,48,1536]{2,1,0:T(8,128)(2,1)} %gather_fusion), calls=%async_computation | async-start | bytes 4718592 | tf_op jit(solution)/shard_map/all_to_all | solution.py:412

commit v3 on v2

--- a/solution.py
+++ b/solution.py
@@ -11,7 +11,7 @@
 TILE = 64
 LANES = 128
 CHUNK = 256
-VMEM_LIMIT = 52 * 1024 * 1024
+MIB = 1024 * 1024
 
 
 def plane(count):
@@ -44,10 +44,14 @@
     def index(a, b, c):
         return (a * short + b) * 2 + c
 
-    def hop(source, slot, way, target):
+    parts = recv.shape[0]
+    depth = own.shape[0] // parts
+
+    def hop(source, part, slot, way, target):
+        at = pl.ds(part * depth, depth)
         return pltpu.make_async_remote_copy(
-            src_ref=source, dst_ref=blocks.at[slot], send_sem=send.at[way, slot],
-            recv_sem=recv.at[slot], device_id={"walk": target}, device_id_type=MESH,
+            src_ref=source.at[at], dst_ref=blocks.at[slot, at], send_sem=send.at[way, part, slot],
+            recv_sem=recv.at[part, slot], device_id={"walk": target}, device_id_type=MESH,
         )
 
     def row_copy(k):
@@ -72,47 +76,53 @@
     spread_z, spread_y = 2 * long - 1, 2 * short - 1
     greet(count, me)
 
-    for way, whether, target in ways(0, 0):
-        @pl.when(whether)
-        def _(way=way, target=target):
-            hop(own, me, way, target).start()
-    hop(own, me, 4, index(z, y, 1 - core)).start()
-
-    @pl.loop(1, count)
-    def _(k):
-        row_copy(k).start()
+    sibling = index(z, y, 1 - core)
+    for part in range(parts):
+        for way, whether, target in ways(0, 0):
+            @pl.when(whether)
+            def _(way=way, target=target):
+                hop(own, part, me, way, target).start()
+        hop(own, part, me, 4, sibling).start()
 
     keep = pltpu.make_async_copy(own, blocks.at[me], own_sem.at[0])
     keep_rows = pltpu.make_async_copy(rows.at[me], shares.at[me], own_sem.at[1])
     keep.start()
     keep_rows.start()
+    row_copy(count - 1).start()
 
     def each(act, start):
-        @pl.loop(start, spread_z * spread_y)
-        def _(k):
+        def body(k, seen):
             dy, dz = signed(k // spread_z), signed(lax.rem(k, spread_z))
             inside = (z + dz >= 0) & (z + dz < long) & (y + dy >= 0) & (y + dy < short)
 
             @pl.when(inside)
             def _():
-                act(dz, dy, index(z + dz, y + dy, core))
-
-    def forward(dz, dy, slot):
-        hop(own, slot, 0, index(z, y, 1 - core)).wait_recv()
-        for way, whether, target in ways(dz, dy):
-            @pl.when(whether)
-            def _(way=way, target=target):
-                hop(blocks.at[slot], slot, way, target).start()
-        hop(blocks.at[slot], slot, 4, index(z, y, 1 - core)).start()
-
-    def finish(dz, dy, slot):
-        for way, whether, target in ways(dz, dy):
-            @pl.when(whether)
-            def _(way=way, target=target):
-                hop(own, slot, way, target).wait_send()
-        hop(own, slot, 4, index(z, y, 1 - core)).wait_send()
+                act(dz, dy, index(z + dz, y + dy, core), seen)
+
+            return seen + jnp.where(inside, 1, 0)
+
+        lax.fori_loop(start, spread_z * spread_y, body, jnp.int32(0))
+
+    def forward(dz, dy, slot, seen):
+        for part in range(parts):
+            hop(own, part, slot, 0, sibling).wait_recv()
+            for way, whether, target in ways(dz, dy):
+                @pl.when(whether)
+                def _(way=way, target=target):
+                    hop(blocks.at[slot], part, slot, way, target).start()
+            hop(blocks.at[slot], part, slot, 4, sibling).start()
+        row_copy(2 * seen + 1).start()
+        row_copy(2 * seen + 2).start()
+
+    def finish(dz, dy, slot, seen):
         other = slot + 1 - 2 * core
-        hop(own, other, 4, index(z, y, 1 - core)).wait_recv()
+        for part in range(parts):
+            for way, whether, target in ways(dz, dy):
+                @pl.when(whether)
+                def _(way=way, target=target):
+                    hop(own, part, slot, way, target).wait_send()
+            hop(own, part, slot, 4, sibling).wait_send()
+            hop(own, part, other, 4, sibling).wait_recv()
 
     each(forward, 1)
     each(finish, 0)
@@ -126,6 +136,7 @@
 
 def exchange(own, rows):
     count = rows.shape[0]
+    parts = 2 if count <= 32 and own.shape[0] % 2 == 0 else 1
     anywhere = pl.BlockSpec(memory_space=pl.ANY)
     return pl.pallas_call(
         functools.partial(exchange_kernel, count),
@@ -137,8 +148,8 @@
         out_specs=(anywhere,) * 2,
         scratch_shapes=[
             pltpu.SemaphoreType.DMA((2,)),
-            pltpu.SemaphoreType.DMA((5, count)),
-            pltpu.SemaphoreType.DMA((count,)),
+            pltpu.SemaphoreType.DMA((5, parts, count)),
+            pltpu.SemaphoreType.DMA((parts, count)),
             pltpu.SemaphoreType.DMA((count,)),
             pltpu.SemaphoreType.DMA((count,)),
         ],
@@ -347,7 +358,7 @@
             ]
             + ([pltpu.VMEM((width, width), jnp.float32)] if move else []),
         ),
-        compiler_params=pltpu.CompilerParams(vmem_limit_bytes=VMEM_LIMIT),
+        compiler_params=pltpu.CompilerParams(vmem_limit_bytes=32 * MIB),
         cost_estimate=pl.CostEstimate(flops=flops, bytes_accessed=2 * chol.size, transcendentals=0),
         name="step",
     )(*places, theta_t, orbitals, chol, fields)
@@ -370,7 +381,7 @@
             out_specs=(whole((width, width)),) * 2,
             scratch_shapes=[pltpu.VMEM((width, width), jnp.float32)] * 2,
         ),
-        compiler_params=pltpu.CompilerParams(vmem_limit_bytes=VMEM_LIMIT),
+        compiler_params=pltpu.CompilerParams(vmem_limit_bytes=38 * MIB),
         cost_estimate=pl.CostEstimate(flops=4 * chol.size, bytes_accessed=2 * chol.size, transcendentals=0),
         name="potentials",
     )(*places, chol, shifts)
@@ -385,7 +396,7 @@
         in_specs=[vmem] * 3,
         out_specs=vmem,
         scratch_shapes=[pltpu.VMEM((occupied, width), jnp.bfloat16)],
-        compiler_params=pltpu.CompilerParams(vmem_limit_bytes=VMEM_LIMIT),
+        compiler_params=pltpu.CompilerParams(vmem_limit_bytes=24 * MIB),
         cost_estimate=pl.CostEstimate(
             flops=4 * occupied * width * width, bytes_accessed=4 * width * width, transcendentals=0
         ),

time: 211 us -> 202 us (0.957)
  Pallas kernels: 170 us -> 144 us
  local copies, waits for them, and re-layouts: 14.9 us -> 34.2 us
  starting transfers between devices: 17.9 us -> 15.4 us
    unnamed x9 -> x25, local copies, waits for them, and re-layouts: 2.54 us -> 21.9 us
    pallas_call x1, Pallas kernels: 94.8 us -> 85.4 us  [exchange(): pl.pallas_call(functools.partial(exchange_kernel, count), out_shape=(jax....]
    pallas_call x2, Pallas kernels: 31.8 us -> 22.7 us  [step(): pl.pallas_call(functools.partial(step_kernel, move), out_shape=(small, sm...]
    pallas_call x1, Pallas kernels: 13.3 us -> 9.71 us  [potentials(): pl.pallas_call(potential_kernel, out_shape=(full, full), grid_spec=pltpu....]
    pallas_call x1, Pallas kernels: 15.3 us -> 12.5 us  [moves(): pl.pallas_call(moves_kernel, out_shape=jax.ShapeDtypeStruct((occupied, wi...]
    all_to_all x1, starting transfers between devices: 17.9 us -> 15.4 us  [local(): lax.all_to_all(chosen, 'walk', split_axis=0, concat_axis=0, tiled=True)]
  transfers between devices with their start and end apart: 1 -> 1, of which waited for: 0 -> 0; matrix products, arithmetic and copies ran while one was open for 4% -> 5% of each run, Pallas kernels for 29% -> 23%
where the time goes in v3:
time: 202 us; the launch traced here: 199 us
  Pallas kernels  144 us (71%)
  local copies, waits for them, and re-layouts  34.2 us (17%)
  starting transfers between devices  15.4 us (8%)
  between operations  2.7 us (1%)
  other arithmetic  2.2 us (1%)
    pallas_call x1, Pallas kernels, exchange(): pl.pallas_call(functools.partial(exchange_kernel, count), out_shape=(jax....  85.4 us
    pallas_call x2, Pallas kernels, step(): pl.pallas_call(functools.partial(step_kernel, move), out_shape=(small, sm...  22.7 us
    unnamed x25, local copies, waits for them, and re-layouts  21.9 us
    all_to_all x1, starting transfers between devices, local(): lax.all_to_all(chosen, 'walk', split_axis=0, concat_axis=0, tiled=True)  15.4 us
    pallas_call x1, Pallas kernels, gather_shifts(): pl.pallas_call(functools.partial(shifts_kernel, count), out_shape=jax.Sha...  13.9 us
    pallas_call x1, Pallas kernels, moves(): pl.pallas_call(moves_kernel, out_shape=jax.ShapeDtypeStruct((occupied, wi...  12.5 us
    pallas_call x1, Pallas kernels, potentials(): pl.pallas_call(potential_kernel, out_shape=(full, full), grid_spec=pltpu....  9.71 us
  transfers between devices with their start and end apart: 1, of which 0 were waited for; matrix products, arithmetic and copies ran while one was open for 5% of the time, Pallas kernels for 23%

profile of v3, /device:TPU:13, one launch (start us, length us, event | category | flops | bytes accessed | tf_op | source)
XLA Modules:
  0.0 198.7 jit_solution(10927006963054823853)
XLA Ops:
  0.6 0.7 pad_clamp_fusion
  1.3 1.4 convert_element_type.7
  2.7 0.8 convert_element_type.8
  3.5 1.1 copy.21
  4.6 1.3 reshape.50.own
  5.9 85.4 %exchange.1 = (bf16[16,8,4,64,128]{4,3,2,1,0:T(8,128)(2,1)}, bf16[16,48,1536]{2,1,0:T(8,128)(2,1)}) custom-call(bf16[8,4,64,128]{3,2,1,0:T(8,128)(2,1)} %reshape.50.own, bf16[16,48,1536]{2,1,0:T(8,128)(2,1)} %bitcast.19), custom_call_target="tpu_custom_call" | custom-call | tf_op jit(solution)/shard_map/exchange/pallas_call | solution.py:141
  91.3 3.8 %gather_fusion = bf16[16,48,1536]{2,1,0:T(8,128)(2,1)} fusion(bf16[16,48,1536]{2,1,0:T(8,128)(2,1)} %get-tuple-element.11, s32[1024]{0:T(1024)S(1)} %pad_clamp_fusion), kind=kCustom, calls=%fused_computation | custom fusion | bytes 4718656 | tf_op jit(solution)/shard_map/jit(_take)/gather | solution.py:422
  95.1 15.4 %all-to-all-start = ((bf16[16,48,1536]{2,1,0:T(8,128)(2,1)}), bf16[16,48,1536]{2,1,0:T(8,128)(2,1)}, u32[]{:S(2)}, u32[]{:S(2)}) async-start(bf16[16,48,1536]{2,1,0:T(8,128)(2,1)} %gather_fusion), calls=%async_computation | async-start | bytes 4718592 | tf_op jit(solution)/shard_map/all_to_all | solution.py:423
  113.9 4.5 %copy.18 = bf16[1,768,1536]{1,2,0:T(8,128)(2,1)} copy(bf16[1,768,1536]{2,1,0:T(8,128)(2,1)} %param.7) | data formatting | bytes 4718592 | tf_op args[1]
  118.4 3.4 %copy-done = bf16[16,8,4,64,128]{4,3,2,1,0:T(8,128)(2,1)S(1)} copy-done((bf16[16,8,4,64,128]{4,3,2,1,0:T(8,128)(2,1)S(1)}, bf16[16,8,4,64,128]{4,3,2,1,0:T(8,128)(2,1)}, u32[]{:S(2)}) %copy-start) | copy-done | bytes 8388632
  121.8 1.7 copy-done.3
  123.5 14.8 %step.2 = (f32[16,8,128]{2,1,0:T(8,128)S(1)}, f32[16,8,128]{2,1,0:T(8,128)S(1)}, bf16[768,1536]{1,0:T(8,128)(2,1)S(1)}) custom-call(s32[64]{0:T(128)S(1)} %get-tuple-element.31.rows_ref, s32[64]{0:T(128)S(1)} %get-tuple-element.30.cols_ref, s32[64]{0:T(128)S(1)} %get-tuple-element.26.odds_ref, bf16[1536,768]{1,0:T(8,128)(2,1)S(1)} %bitcast.21, ...), custom_call_target="tpu_custom_call" | custom-call | flops 7247757312 | bytes 8388608 | tf_op jit(solution)/shard_map/step/pallas_call | solution.py:342
  138.3 3.4 %copy-done.1 = bf16[16,8,4,64,128]{4,3,2,1,0:T(8,128)(2,1)S(1)} copy-done((bf16[16,8,4,64,128]{4,3,2,1,0:T(8,128)(2,1)S(1)}, bf16[16,8,4,64,128]{4,3,2,1,0:T(8,128)(2,1)}, u32[]{:S(2)}) %copy-start.1) | copy-done | bytes 8388632
  141.7 7.9 %step.3 = (f32[16,8,128]{2,1,0:T(8,128)S(1)}, f32[16,8,128]{2,1,0:T(8,128)S(1)}) custom-call(s32[64]{0:T(128)S(1)} %get-tuple-element.31.rows_ref, s32[64]{0:T(128)S(1)} %get-tuple-element.30.cols_ref, s32[64]{0:T(128)S(1)} %get-tuple-element.26.odds_ref, bf16[1536,768]{1,0:T(8,128)(2,1)S(1)} %bitcast.22, bf16[768,1536]{1,0:T(8,128)(2,1)S(1)} %get-tuple-element.14.orbitals, ...), custom_call_target="tpu_custom_call" | custom-call | flops 3623878656 | bytes 8388608 | tf_op jit(solution)/shard_map/step/pallas_call | solution.py:342
  149.9 0.7 reshape.53.own
  150.8 0.7 reshape.65
  151.6 13.9 %gather_shifts.1 = f32[16,2,256]{2,1,0:T(2,128)} custom-call(f32[2,256]{1,0:T(2,128)} %reshape.53.own), custom_call_target="tpu_custom_call" | custom-call | tf_op jit(solution)/shard_map/gather_shifts/pallas_call | solution.py:187
  166.0 0.7 constant_dynamic-slice_fusion
  167.4 9.7 %potentials.1 = (bf16[1536,1536]{1,0:T(8,128)(2,1)S(1)}, bf16[1536,1536]{1,0:T(8,128)(2,1)S(1)}) custom-call(s32[64]{0:T(128)S(1)} %get-tuple-element.31.rows_ref, s32[64]{0:T(128)S(1)} %get-tuple-element.30.cols_ref, s32[64]{0:T(128)S(1)} %get-tuple-element.26.odds_ref, bf16[16,8,4,64,128]{4,3,2,1,0:T(8,128)(2,1)} %get-tuple-element.12.chol, ...), custom_call_target="tpu_custom_call" | custom-call | flops 16777216 | bytes 8388608 | tf_op jit(solution)/shard_map/potentials/pallas_call | solution.py:371
  177.1 2.2 %copy-done.5 = bf16[1536,1536]{1,0:T(8,128)(2,1)} copy-done((bf16[1536,1536]{1,0:T(8,128)(2,1)}, bf16[1536,1536]{1,0:T(8,128)(2,1)S(1)}, u32[]{:S(2)}) %copy-start.5) | copy-done | bytes 4718616
  179.3 2.2 %copy-done.7 = bf16[1536,1536]{1,0:T(8,128)(2,1)} copy-done((bf16[1536,1536]{1,0:T(8,128)(2,1)}, bf16[1536,1536]{1,0:T(8,128)(2,1)S(1)}, u32[]{:S(2)}) %copy-start.7) | copy-done | bytes 4718616
  181.5 2.3 %copy-done.6 = bf16[1536,1536]{1,0:T(8,128)(2,1)S(1)} copy-done((bf16[1536,1536]{1,0:T(8,128)(2,1)S(1)}, bf16[1536,1536]{1,0:T(8,128)(2,1)}, u32[]{:S(2)}) %copy-start.6) | copy-done | bytes 4718616
  183.8 2.3 %copy-done.8 = bf16[1536,1536]{1,0:T(8,128)(2,1)S(1)} copy-done((bf16[1536,1536]{1,0:T(8,128)(2,1)S(1)}, bf16[1536,1536]{1,0:T(8,128)(2,1)}, u32[]{:S(2)}) %copy-start.8) | copy-done | bytes 4718616
  186.2 12.5 %moves.1 = bf16[768,1536]{1,0:T(8,128)(2,1)} custom-call(bf16[768,1536]{1,0:T(8,128)(2,1)} %bitcast.2.orbitals, bf16[1536,1536]{1,0:T(8,128)(2,1)S(1)} %copy-done.6, bf16[1536,1536]{1,0:T(8,128)(2,1)S(1)} %copy-done.8), custom_call_target="tpu_custom_call" | custom-call | flops 7247757312 | bytes 9437184 | tf_op jit(solution)/shard_map/moves/pallas_call | solution.py:393
  (43 shorter events, 3.4 us)
Async XLA Ops:
  95.1 15.4 %copy-start.11 = (s32[16]{0:T(128)S(1)}, s32[16]{0:T(128)}, u32[]{:S(2)}) copy-start(s32[16]{0:T(128)} %param.11) | copy-start | bytes 196
  95.1 17.3 %copy-start.9 = (s32[16,4]{0,1:T(4,128)S(1)}, s32[16,4]{0,1:T(4,128)}, u32[]{:S(2)}) copy-start(s32[16,4]{0,1:T(4,128)} %param.9) | copy-start | bytes 772
  95.1 17.8 %copy-start.10 = (f32[2,1,256]{2,1,0:T(1,128)S(1)}, f32[2,1,256]{2,1,0:T(1,128)}, u32[]{:S(2)}) copy-start(f32[2,1,256]{2,1,0:T(1,128)} %param.10) | copy-start | bytes 6148
  95.1 86.4 %all-to-all-start = ((bf16[16,48,1536]{2,1,0:T(8,128)(2,1)}), bf16[16,48,1536]{2,1,0:T(8,128)(2,1)}, u32[]{:S(2)}, u32[]{:S(2)}) async-start(bf16[16,48,1536]{2,1,0:T(8,128)(2,1)} %gather_fusion), calls=%async_computation | async-start | bytes 4718592 | tf_op jit(solution)/shard_map/all_to_all | solution.py:423
  113.9 4.5 %copy-start.2 = (bf16[1,768,1536]{2,1,0:T(8,128)(2,1)S(1)}, bf16[1,768,1536]{2,1,0:T(8,128)(2,1)}, u32[]{:S(2)}) copy-start(bf16[1,768,1536]{2,1,0:T(8,128)(2,1)} %param.6) | copy-start | bytes 7077892
  118.4 3.4 %copy-start = (bf16[16,8,4,64,128]{4,3,2,1,0:T(8,128)(2,1)S(1)}, bf16[16,8,4,64,128]{4,3,2,1,0:T(8,128)(2,1)}, u32[]{:S(2)}) copy-start(bf16[16,8,4,64,128]{4,3,2,1,0:T(8,128)(2,1)} %get-tuple-element.12.chol) | copy-start | bytes 25165828
  121.8 1.7 copy-start.3
  123.5 14.8 %copy-start.4 = (bf16[1,768,1536]{1,2,0:T(8,128)(2,1)S(1)}, bf16[1,768,1536]{1,2,0:T(8,128)(2,1)}, u32[]{:S(2)}) copy-start(bf16[1,768,1536]{1,2,0:T(8,128)(2,1)} %copy.18) | copy-start | bytes 7077892
  138.3 3.4 %copy-start.1 = (bf16[16,8,4,64,128]{4,3,2,1,0:T(8,128)(2,1)S(1)}, bf16[16,8,4,64,128]{4,3,2,1,0:T(8,128)(2,1)}, u32[]{:S(2)}) copy-start(bf16[16,8,4,64,128]{4,3,2,1,0:T(8,128)(2,1)} %get-tuple-element.12.chol) | copy-start | bytes 25165828
  177.1 2.2 %copy-start.5 = (bf16[1536,1536]{1,0:T(8,128)(2,1)}, bf16[1536,1536]{1,0:T(8,128)(2,1)S(1)}, u32[]{:S(2)}) copy-start(bf16[1536,1536]{1,0:T(8,128)(2,1)S(1)} %get-tuple-element.16.first) | copy-start | bytes 14155780
  179.3 2.2 %copy-start.7 = (bf16[1536,1536]{1,0:T(8,128)(2,1)}, bf16[1536,1536]{1,0:T(8,128)(2,1)S(1)}, u32[]{:S(2)}) copy-start(bf16[1536,1536]{1,0:T(8,128)(2,1)S(1)} %get-tuple-element.17.second) | copy-start | bytes 14155780
  181.5 2.3 %copy-start.6 = (bf16[1536,1536]{1,0:T(8,128)(2,1)S(1)}, bf16[1536,1536]{1,0:T(8,128)(2,1)}, u32[]{:S(2)}) copy-start(bf16[1536,1536]{1,0:T(8,128)(2,1)} %copy-done.5) | copy-start | bytes 14155780
  183.8 2.3 %copy-start.8 = (bf16[1536,1536]{1,0:T(8,128)(2,1)S(1)}, bf16[1536,1536]{1,0:T(8,128)(2,1)}, u32[]{:S(2)}) copy-start(bf16[1536,1536]{1,0:T(8,128)(2,1)} %copy-done.7) | copy-start | bytes 14155780

commit v4 on v3

--- a/solution.py
+++ b/solution.py
@@ -54,7 +54,11 @@
             recv_sem=recv.at[part, slot], device_id={"walk": target}, device_id_type=MESH,
         )
 
-    def row_copy(k):
+    def signed(k):
+        return jnp.where(lax.rem(k, 2) == 1, (k + 1) // 2, -(k // 2))
+
+    def row_copy(j):
+        k = count // 2 + signed(j)
         target = lax.rem(me + k, count)
         return pltpu.make_async_remote_copy(
             src_ref=rows.at[target], dst_ref=shares.at[me], send_sem=row_send.at[k],
@@ -70,9 +74,6 @@
             (3, (dy >= 0) & (y > 0), index(z, y - 1, core)),
         )
 
-    def signed(k):
-        return jnp.where(lax.rem(k, 2) == 1, (k + 1) // 2, -(k // 2))
-
     spread_z, spread_y = 2 * long - 1, 2 * short - 1
     greet(count, me)
 
@@ -88,7 +89,12 @@
     keep_rows = pltpu.make_async_copy(rows.at[me], shares.at[me], own_sem.at[1])
     keep.start()
     keep_rows.start()
-    row_copy(count - 1).start()
+    batch = (count - 1) // long
+    early = count - 1 - batch * (long - 1)
+
+    @pl.loop(0, early)
+    def _(j):
+        row_copy(j).start()
 
     def each(act, start):
         def body(k, seen):
@@ -111,8 +117,12 @@
                 def _(way=way, target=target):
                     hop(blocks.at[slot], part, slot, way, target).start()
             hop(blocks.at[slot], part, slot, 4, sibling).start()
-        row_copy(2 * seen + 1).start()
-        row_copy(2 * seen + 2).start()
+
+        @pl.when(seen < long - 1)
+        def _():
+            @pl.loop(0, batch)
+            def _(j):
+                row_copy(early + seen * batch + j).start()
 
     def finish(dz, dy, slot, seen):
         other = slot + 1 - 2 * core
@@ -129,9 +139,9 @@
     keep.wait()
     keep_rows.wait()
 
-    @pl.loop(1, count)
-    def _(k):
-        row_copy(k).wait()
+    @pl.loop(0, count - 1)
+    def _(j):
+        row_copy(j).wait()
 
 
 def exchange(own, rows):
@@ -223,7 +233,7 @@
     potential[at] = potential[at] + jnp.where(keep, total, 0.0)
 
 
-def step_kernel(move, rows_ref, cols_ref, odds_ref, theta_t, orbitals, chol, fields, *rest):
+def step_kernel(move, rows_ref, cols_ref, odds_ref, theta, orbitals, chol, fields, *rest):
     if move:
         bias_ref, shift_ref, out, green, sums, potential = rest
     else:
@@ -237,8 +247,9 @@
         @pl.loop(0, width // CHUNK)
         def _(i):
             at = pl.ds(pl.multiple_of(i * CHUNK, CHUNK), CHUNK)
-            green[:, at] = jnp.dot(
-                theta_t[...], orbitals[:, at], preferred_element_type=jnp.float32
+            green[:, at] = lax.dot_general(
+                theta[...], orbitals[:, at], (((0,), (0,)), ((), ())),
+                preferred_element_type=jnp.float32,
             ).astype(green.dtype)
             if move:
                 potential[:, at] = jnp.zeros((potential.shape[0], CHUNK), jnp.float32)
@@ -283,7 +294,7 @@
                 out[:, at] = (orbitals[:, at].astype(jnp.float32) + moved).astype(out.dtype)
 
 
-def potential_kernel(rows_ref, cols_ref, odds_ref, chol, shifts, out1, out2, one, two):
+def moves_kernel(rows_ref, cols_ref, odds_ref, chol, shifts, orbitals, out, one, two, mid):
     now = pl.program_id(0)
     blocks, pairs, slots = chol.shape[:3]
     width = one.shape[1]
@@ -305,34 +316,27 @@
             add_tile(one, *place, shifts[0, b], block)
             add_tile(two, *place, shifts[1, b], block)
 
-    @pl.when(now == pl.num_programs(0) - 1)
-    def _():
-        @pl.loop(0, width // CHUNK)
-        def _(i):
-            at = pl.ds(pl.multiple_of(i * CHUNK, CHUNK), CHUNK)
-            out1[:, at] = one[:, at].astype(out1.dtype)
-            out2[:, at] = two[:, at].astype(out2.dtype)
-
-
-def moves_kernel(orbitals, first, second, out, mid):
-    width = orbitals.shape[1]
-
     def move(source, potential, target):
         @pl.loop(0, width // CHUNK)
         def _(i):
             at = pl.ds(pl.multiple_of(i * CHUNK, CHUNK), CHUNK)
-            moved = jnp.dot(source[...], potential[:, at], preferred_element_type=jnp.float32)
+            moved = jnp.dot(
+                source[...], potential[:, at].astype(jnp.bfloat16),
+                preferred_element_type=jnp.float32,
+            )
             target[:, at] = (source[:, at].astype(jnp.float32) + moved).astype(target.dtype)
 
-    move(orbitals, first, mid)
-    move(mid, second, out)
+    @pl.when(now == pl.num_programs(0) - 1)
+    def _():
+        move(orbitals, one, mid)
+        move(mid, two, out)
 
 
 def whole(shape):
     return pl.BlockSpec(shape, lambda i, *_: (0,) * len(shape), pipeline_mode=pl.Buffered(1))
 
 
-def step(move, places, theta_t, orbitals, chol, fields):
+def step(move, places, theta, orbitals, chol, fields):
     count, pairs, slots = chol.shape[:3]
     occupied, width = orbitals.shape
     per = 4 if count % 4 == 0 else 1
@@ -346,7 +350,7 @@
             num_scalar_prefetch=3,
             grid=(count // per,),
             in_specs=[
-                whole((width, occupied)),
+                whole((occupied, width)),
                 whole((occupied, width)),
                 pl.BlockSpec((per, pairs, slots, TILE, LANES), lambda i, *_: (i, 0, 0, 0, 0)),
                 lanes,
@@ -361,47 +365,34 @@
         compiler_params=pltpu.CompilerParams(vmem_limit_bytes=32 * MIB),
         cost_estimate=pl.CostEstimate(flops=flops, bytes_accessed=2 * chol.size, transcendentals=0),
         name="step",
-    )(*places, theta_t, orbitals, chol, fields)
-
-
-def potentials(places, chol, shifts, width):
+    )(*places, theta, orbitals, chol, fields)
+
+
+def moves(places, chol, shifts, orbitals):
     count, pairs, slots = chol.shape[:3]
+    occupied, width = orbitals.shape
     per = 4 if count % 4 == 0 else 1
-    full = jax.ShapeDtypeStruct((width, width), jnp.bfloat16)
     return pl.pallas_call(
-        potential_kernel,
-        out_shape=(full, full),
+        moves_kernel,
+        out_shape=jax.ShapeDtypeStruct((occupied, width), jnp.bfloat16),
         grid_spec=pltpu.PrefetchScalarGridSpec(
             num_scalar_prefetch=3,
             grid=(count // per,),
             in_specs=[
                 pl.BlockSpec((per, pairs, slots, TILE, LANES), lambda i, *_: (i, 0, 0, 0, 0)),
                 pl.BlockSpec((2, per, pairs, LANES), lambda i, *_: (0, i, 0, 0)),
+                whole((occupied, width)),
             ],
-            out_specs=(whole((width, width)),) * 2,
-            scratch_shapes=[pltpu.VMEM((width, width), jnp.float32)] * 2,
+            out_specs=whole((occupied, width)),
+            scratch_shapes=[pltpu.VMEM((width, width), jnp.float32)] * 2
+            + [pltpu.VMEM((occupied, width), jnp.bfloat16)],
         ),
         compiler_params=pltpu.CompilerParams(vmem_limit_bytes=38 * MIB),
-        cost_estimate=pl.CostEstimate(flops=4 * chol.size, bytes_accessed=2 * chol.size, transcendentals=0),
-        name="potentials",
-    )(*places, chol, shifts)
-
-
-def moves(orbitals, first, second):
-    occupied, width = orbitals.shape
-    vmem = pl.BlockSpec(memory_space=pltpu.VMEM)
-    return pl.pallas_call(
-        moves_kernel,
-        out_shape=jax.ShapeDtypeStruct((occupied, width), jnp.bfloat16),
-        in_specs=[vmem] * 3,
-        out_specs=vmem,
-        scratch_shapes=[pltpu.VMEM((occupied, width), jnp.bfloat16)],
-        compiler_params=pltpu.CompilerParams(vmem_limit_bytes=24 * MIB),
         cost_estimate=pl.CostEstimate(
-            flops=4 * occupied * width * width, bytes_accessed=4 * width * width, transcendentals=0
+            flops=4 * occupied * width * width, bytes_accessed=2 * chol.size, transcendentals=0
         ),
         name="moves",
-    )(orbitals, first, second)
+    )(*places, chol, shifts, orbitals)
 
 
 def spread(values, vectors):
@@ -426,18 +417,16 @@
     flat = tiles.reshape(-1)
     row, col = flat // tile_rows, flat % tile_rows
     places = (row * TILE, (col // 2) * LANES, col % 2)
-    theta_t = theta[0].T
     drive = spread(fields[:, 0], vectors)
-    bias1, shift1, orbitals = step(True, places, theta_t, walkers[0], chol, drive[0])
-    bias2, shift2 = step(False, places, theta_t, orbitals, chol, drive[1])
+    bias1, shift1, orbitals = step(True, places, theta[0], walkers[0], chol, drive[0])
+    bias2, shift2 = step(False, places, theta[0], orbitals, chol, drive[1])
     biases = jnp.stack([bias1, bias2])[..., ::TILE].reshape(2, 1, -1)
     own_shift = jnp.stack([shift1, shift2])[..., ::TILE].reshape(2, -1)
     all_shifts = gather_shifts(own_shift, count)
     me = lax.axis_index("walk")
     mine = lax.dynamic_index_in_dim(source, me, 0, keepdims=False)
     chosen_shift = lax.dynamic_index_in_dim(all_shifts, mine, 0, keepdims=False)
-    first, second = potentials(places, chol, spread(chosen_shift, vectors), width)
-    return (moves(origin, first, second)[None], biases)
+    return (moves(places, chol, spread(chosen_shift, vectors), origin)[None], biases)
 
 
 def solution(mesh):

time: 202 us -> 196 us (0.970)
  local copies, waits for them, and re-layouts: 34.2 us -> 20.7 us
  Pallas kernels: 144 us -> 150 us
  starting transfers between devices: 15.4 us -> 18.2 us
    unnamed x25 -> x16, local copies, waits for them, and re-layouts: 21.9 us -> 8.45 us
    pallas_call x1 -> x0, Pallas kernels: 9.71 us -> none  [potentials(): pl.pallas_call(potential_kernel, out_shape=(full, full), grid_spec=pltpu....]
    pallas_call x1, Pallas kernels: 13.9 us -> 21.1 us  [gather_shifts(): pl.pallas_call(functools.partial(shifts_kernel, count), out_shape=jax.Sha...]
    pallas_call x1, Pallas kernels: 12.5 us -> 18.9 us  [moves(): pl.pallas_call(moves_kernel, out_shape=jax.ShapeDtypeStruct((occupied, wi...]
    all_to_all x1, starting transfers between devices: 15.4 us -> 18.2 us  [local(): lax.all_to_all(chosen, 'walk', split_axis=0, concat_axis=0, tiled=True)]
  transfers between devices with their start and end apart: 1 -> 1, of which waited for: 0 -> 0; matrix products, arithmetic and copies ran while one was open for 5% -> 3% of each run, Pallas kernels for 23% -> 23%
where the time goes in v4:
time: 196 us; the launch traced here: 193 us
  Pallas kernels  150 us (77%)
  local copies, waits for them, and re-layouts  20.7 us (11%)
  starting transfers between devices  18.2 us (9%)
  between operations  2.51 us (1%)
    pallas_call x1, Pallas kernels, exchange(): pl.pallas_call(functools.partial(exchange_kernel, count), out_shape=(jax....  86.4 us
    pallas_call x2, Pallas kernels, step(): pl.pallas_call(functools.partial(step_kernel, move), out_shape=(small, sm...  23.5 us
    pallas_call x1, Pallas kernels, gather_shifts(): pl.pallas_call(functools.partial(shifts_kernel, count), out_shape=jax.Sha...  21.1 us
    pallas_call x1, Pallas kernels, moves(): pl.pallas_call(moves_kernel, out_shape=jax.ShapeDtypeStruct((occupied, wi...  18.9 us
    all_to_all x1, starting transfers between devices, local(): lax.all_to_all(chosen, 'walk', split_axis=0, concat_axis=0, tiled=True)  18.2 us
    unnamed x16, local copies, waits for them, and re-layouts  8.45 us
  transfers between devices with their start and end apart: 1, of which 0 were waited for; matrix products, arithmetic and copies ran while one was open for 3% of the time, Pallas kernels for 23%

profile of v4, /device:TPU:13, one launch (start us, length us, event | category | flops | bytes accessed | tf_op | source)
XLA Modules:
  0.0 192.9 jit_solution(13757728830619736187)
XLA Ops:
  0.6 1.4 convert_element_type.7
  2.1 0.8 convert_element_type.8
  2.9 1.1 copy.19
  4.0 1.3 reshape.50.own
  5.3 86.4 %exchange.1 = (bf16[16,8,4,64,128]{4,3,2,1,0:T(8,128)(2,1)}, bf16[16,48,1536]{2,1,0:T(8,128)(2,1)}) custom-call(bf16[8,4,64,128]{3,2,1,0:T(8,128)(2,1)} %reshape.50.own, bf16[16,48,1536]{2,1,0:T(8,128)(2,1)} %bitcast.17), custom_call_target="tpu_custom_call" | custom-call | tf_op jit(solution)/shard_map/exchange/pallas_call | solution.py:151
  91.7 3.8 %gather_fusion = bf16[16,48,1536]{2,1,0:T(8,128)(2,1)} fusion(bf16[16,48,1536]{2,1,0:T(8,128)(2,1)} %get-tuple-element.13, s32[1024]{0:T(1024)S(1)} %pad_clamp_fusion), kind=kCustom, calls=%fused_computation | custom fusion | bytes 4718656 | tf_op jit(solution)/shard_map/jit(_take)/gather | solution.py:413
  95.5 18.2 %all-to-all-start = ((bf16[16,48,1536]{2,1,0:T(8,128)(2,1)}), bf16[16,48,1536]{2,1,0:T(8,128)(2,1)}, u32[]{:S(2)}, u32[]{:S(2)}) async-start(bf16[16,48,1536]{2,1,0:T(8,128)(2,1)} %gather_fusion), calls=%async_computation | async-start | bytes 4718592 | tf_op jit(solution)/shard_map/all_to_all | solution.py:414
  113.7 0.6 dynamic_slice.8
  116.2 0.2 broadcast_in_dim.25
  116.6 0.2 broadcast_in_dim.27
  117.0 3.4 %copy-done.1 = bf16[16,8,4,64,128]{4,3,2,1,0:T(8,128)(2,1)S(1)} copy-done((bf16[16,8,4,64,128]{4,3,2,1,0:T(8,128)(2,1)S(1)}, bf16[16,8,4,64,128]{4,3,2,1,0:T(8,128)(2,1)}, u32[]{:S(2)}) %copy-start.1) | copy-done | bytes 8388632
  120.4 1.7 copy-done.3
  122.1 15.3 %step.2 = (f32[16,8,128]{2,1,0:T(8,128)S(1)}, f32[16,8,128]{2,1,0:T(8,128)S(1)}, bf16[768,1536]{1,0:T(8,128)(2,1)S(1)}) custom-call(s32[64]{0:T(128)S(1)} %get-tuple-element.27.rows_ref, s32[64]{0:T(128)S(1)} %get-tuple-element.26.cols_ref, s32[64]{0:T(128)S(1)} %get-tuple-element.22.odds_ref, bf16[768,1536]{1,0:T(8,128)(2,1)S(1)} %bitcast.23, ...), custom_call_target="tpu_custom_call" | custom-call | flops 7247757312 | bytes 8388608 | tf_op jit(solution)/shard_map/step/pallas_call | solution.py:346
  137.4 8.2 %step.3 = (f32[16,8,128]{2,1,0:T(8,128)S(1)}, f32[16,8,128]{2,1,0:T(8,128)S(1)}) custom-call(s32[64]{0:T(128)S(1)} %get-tuple-element.27.rows_ref, s32[64]{0:T(128)S(1)} %get-tuple-element.26.cols_ref, s32[64]{0:T(128)S(1)} %get-tuple-element.22.odds_ref, bf16[768,1536]{1,0:T(8,128)(2,1)S(1)} %bitcast.24, bf16[768,1536]{1,0:T(8,128)(2,1)S(1)} %get-tuple-element.11.orbitals, ...), custom_call_target="tpu_custom_call" | custom-call | flops 3623878656 | bytes 8388608 | tf_op jit(solution)/shard_map/step/pallas_call | solution.py:346
  145.6 0.2 slice.27
  145.9 0.7 reshape.65
  146.6 0.2 slice.26
  146.9 0.7 reshape.52.own
  147.6 21.1 %gather_shifts.1 = f32[16,2,256]{2,1,0:T(2,128)} custom-call(f32[2,256]{1,0:T(2,128)} %reshape.52.own), custom_call_target="tpu_custom_call" | custom-call | tf_op jit(solution)/shard_map/gather_shifts/pallas_call | solution.py:197
  169.2 0.7 constant_dynamic-slice_fusion
  170.1 0.3 broadcast_in_dim.30
  170.4 0.2 reshape.53.shifts
  170.6 3.4 %copy-done.2 = bf16[16,8,4,64,128]{4,3,2,1,0:T(8,128)(2,1)S(1)} copy-done((bf16[16,8,4,64,128]{4,3,2,1,0:T(8,128)(2,1)S(1)}, bf16[16,8,4,64,128]{4,3,2,1,0:T(8,128)(2,1)}, u32[]{:S(2)}) %copy-start.2) | copy-done | bytes 8388632
  174.0 18.9 %moves.1 = bf16[768,1536]{1,0:T(8,128)(2,1)} custom-call(s32[64]{0:T(128)S(1)} %get-tuple-element.27.rows_ref, s32[64]{0:T(128)S(1)} %get-tuple-element.26.cols_ref, s32[64]{0:T(128)S(1)} %get-tuple-element.22.odds_ref, bf16[16,8,4,64,128]{4,3,2,1,0:T(8,128)(2,1)S(1)} %copy-done.2, f32[2,16,8,128]{3,2,1,0:T(8,128)S(1)} %reshape.53.shifts, ...), custom_call_target="tpu_custom_call" | custom-call | flops 7247757312 | bytes 8388608 | tf_op jit(solution)/shard_map/moves/pallas_call | solution.py:375
  (33 shorter events, 1.4 us)
Async XLA Ops:
  2.1 3.2 %copy-start.7 = (s32[16]{0:T(128)S(1)}, s32[16]{0:T(128)}, u32[]{:S(2)}) copy-start(s32[16]{0:T(128)} %param.11) | copy-start | bytes 196
  95.5 20.0 %copy-start.5 = (s32[16,4]{0,1:T(4,128)S(1)}, s32[16,4]{0,1:T(4,128)}, u32[]{:S(2)}) copy-start(s32[16,4]{0,1:T(4,128)} %param.9) | copy-start | bytes 772
  95.5 20.5 %copy-start.6 = (f32[2,1,256]{2,1,0:T(1,128)S(1)}, f32[2,1,256]{2,1,0:T(1,128)}, u32[]{:S(2)}) copy-start(f32[2,1,256]{2,1,0:T(1,128)} %param.10) | copy-start | bytes 6148
  95.5 21.5 %copy-start = (bf16[1,768,1536]{2,1,0:T(8,128)(2,1)S(1)}, bf16[1,768,1536]{2,1,0:T(8,128)(2,1)}, u32[]{:S(2)}) copy-start(bf16[1,768,1536]{2,1,0:T(8,128)(2,1)} %param.6) | copy-start | bytes 7077892
  95.5 75.1 %all-to-all-start = ((bf16[16,48,1536]{2,1,0:T(8,128)(2,1)}), bf16[16,48,1536]{2,1,0:T(8,128)(2,1)}, u32[]{:S(2)}, u32[]{:S(2)}) async-start(bf16[16,48,1536]{2,1,0:T(8,128)(2,1)} %gather_fusion), calls=%async_computation | async-start | bytes 4718592 | tf_op jit(solution)/shard_map/all_to_all | solution.py:414
  117.0 3.4 %copy-start.1 = (bf16[16,8,4,64,128]{4,3,2,1,0:T(8,128)(2,1)S(1)}, bf16[16,8,4,64,128]{4,3,2,1,0:T(8,128)(2,1)}, u32[]{:S(2)}) copy-start(bf16[16,8,4,64,128]{4,3,2,1,0:T(8,128)(2,1)} %get-tuple-element.9.chol) | copy-start | bytes 25165828
  120.4 1.7 copy-start.3
  122.1 15.3 %copy-start.4 = (bf16[1,768,1536]{2,1,0:T(8,128)(2,1)S(1)}, bf16[1,768,1536]{2,1,0:T(8,128)(2,1)}, u32[]{:S(2)}) copy-start(bf16[1,768,1536]{2,1,0:T(8,128)(2,1)} %param.7) | copy-start | bytes 7077892
  170.6 3.4 %copy-start.2 = (bf16[16,8,4,64,128]{4,3,2,1,0:T(8,128)(2,1)S(1)}, bf16[16,8,4,64,128]{4,3,2,1,0:T(8,128)(2,1)}, u32[]{:S(2)}) copy-start(bf16[16,8,4,64,128]{4,3,2,1,0:T(8,128)(2,1)} %get-tuple-element.9.chol) | copy-start | bytes 25165828
